TPU v7x, 128 devices: a whole 4x4x4 slice. The times are simulated.
128 devices in a mesh: dp: 64 (over x, y_lo, z, core), ctx: 2 (over y_hi).
Axes of the slice: x: 4, y: 4 (y_hi: 2, y_lo: 2; y = y_hi * 2 + y_lo), z: 4, core: 2. Of those that a mesh axis runs over, the one named last changes fastest.
Arguments:
- tokens: bfloat16 [16384, 896], P(('dp', 'ctx')), may hold values from -6 to 6
- segments: int32 [16384], P(('dp', 'ctx')), may hold values from 0 to 1, as said below
- gain_attn: bfloat16 [896], P(('dp', 'ctx')), may hold values from 0.5 to 1.5
- w_query: bfloat16 [896, 896], P(('dp', 'ctx')), may hold values from -0.1875 to 0.1875
- w_key: bfloat16 [896, 128], P(('dp', 'ctx')), may hold values from -0.1875 to 0.1875
- w_value: bfloat16 [896, 128], P(('dp', 'ctx')), may hold values from -0.1875 to 0.1875
- bias_qkv: bfloat16 [1152], P(('dp', 'ctx')), may hold values from -3 to 3
- w_out: bfloat16 [896, 896], P(('dp', 'ctx')), may hold values from -0.75 to 0.75
- gain_ffn: bfloat16 [896], P(('dp', 'ctx')), may hold values from 0.5 to 1.5
- w_gate: bfloat16 [896, 4864], P(('dp', 'ctx')), may hold values from -0.1875 to 0.1875
- w_up: bfloat16 [896, 4864], P(('dp', 'ctx')), may hold values from -0.1875 to 0.1875
- w_down: bfloat16 [4864, 896], P(('dp', 'ctx')), may hold values from -0.078125 to 0.078125
- cotangent: bfloat16 [16384, 896], P(('dp', 'ctx')), may hold values from -6 to 6
Outputs:
- output: bfloat16 [16384, 896], P(('dp', 'ctx'))
- input_grad: bfloat16 [16384, 896], P(('dp', 'ctx'))
- grad_gain_attn: float32 [896], P(('dp', 'ctx'))
- grad_w_query: float32 [896, 896], P(('dp', 'ctx'))
- grad_w_key: float32 [896, 128], P(('dp', 'ctx'))
- grad_w_value: float32 [896, 128], P(('dp', 'ctx'))
- grad_bias_qkv: float32 [1152], P(('dp', 'ctx'))
- grad_w_out: float32 [896, 896], P(('dp', 'ctx'))
- grad_gain_ffn: float32 [896], P(('dp', 'ctx'))
- grad_w_gate: float32 [896, 4864], P(('dp', 'ctx'))
- grad_w_up: float32 [896, 4864], P(('dp', 'ctx'))
- grad_w_down: float32 [4864, 896], P(('dp', 'ctx'))
Inputs may be any that keep to these rules, and one draw needn't show every extreme that they name: `segments`: in each sequence of 256 consecutive tokens the numbers are 0, then 1, each in one non-empty run; the run of 1 begins at an index from 32 to 224.
All inputs are finite; a program needn't handle non-finite values.
Results may differ from a plain program's by a relative error of at most 0.017.
Values may be sent and summed in bfloat16 or wider, within the bound.
A program may use at most 192 MiB of HBM per device.

v0:
```python
import jax
import jax.numpy as jnp
from jax import lax
from jax.sharding import PartitionSpec as P

HEADS = 14
KV_HEADS = 2
HEAD = 64


epsilon = 1e-06
masked_value = -1000000000.0
rope_base = 1000000.0


def matmul(left_side, right_side):
    return jnp.dot(left_side, right_side, preferred_element_type=jnp.float32)


def matmul_nt(left_side, right_side):
    return lax.dot_general(
        left_side, right_side, (((1,), (1,)), ((), ())), preferred_element_type=jnp.float32
    )


def matmul_tn(left_side, right_side):
    return lax.dot_general(
        left_side, right_side, (((0,), (0,)), ((), ())), preferred_element_type=jnp.float32
    )


def rotary_tables(places):
    half_width = HEAD // 2
    frequency = rope_base ** (-2.0 * jnp.arange(half_width, dtype=jnp.float32) / HEAD)
    angles = places.astype(jnp.float32)[:, None] * frequency[None, :]
    return (jnp.cos(angles)[:, None, :], jnp.sin(angles)[:, None, :])


def rotate(values, cosine, sine_part):
    half_width = values.shape[-1] // 2
    front_half = values[..., :half_width]
    back_half = values[..., half_width:]
    return jnp.concatenate(
        [front_half * cosine - back_half * sine_part, back_half * cosine + front_half * sine_part],
        axis=-1,
    )


def rotate_back(gradient, cosine, sine_part):
    half_width = gradient.shape[-1] // 2
    front_half = gradient[..., :half_width]
    back_half = gradient[..., half_width:]
    return jnp.concatenate(
        [front_half * cosine + back_half * sine_part, back_half * cosine - front_half * sine_part],
        axis=-1,
    )


def normalize(values, gain_vector):
    inverse = lax.rsqrt(jnp.mean(values * values, axis=-1, keepdims=True) + epsilon)
    return (inverse, values * inverse * gain_vector.astype(jnp.float32)[None, :])


def normalize_back(values, inverse, gain_vector, upstream):
    gain_grad = jnp.sum(upstream * values * inverse, axis=0)
    scaled = upstream * gain_vector.astype(jnp.float32)[None, :]
    inner_mean = jnp.mean(scaled * values, axis=-1, keepdims=True)
    return (gain_grad, inverse * scaled - values * inverse * inverse * inverse * inner_mean)


def attention_logits(query_grouped, key_grouped, allowed):
    raw_scores = jnp.einsum(
        "qkgd,lkd->kgql", query_grouped, key_grouped, preferred_element_type=jnp.float32
    )
    return jnp.where(allowed[None, None], raw_scores * HEAD ** (-0.5), masked_value)


def per_device(
    tokens,
    segments,
    gain_attn,
    w_query,
    w_key,
    w_value,
    bias_qkv,
    w_out,
    gain_ffn,
    w_gate,
    w_up,
    w_down,
    cotangent,
):
    row_count = tokens.shape[0]
    width = tokens.shape[1]
    group_width = HEADS // KV_HEADS
    kv_width = KV_HEADS * HEAD
    whole_ids = lax.all_gather(segments, "ctx", axis=0, tiled=True)
    seq_length = whole_ids.shape[0]
    offset = lax.axis_index("ctx") * row_count
    own_place = offset + jnp.arange(row_count, dtype=jnp.int32)
    before = jnp.sum((whole_ids[None, :] < segments[:, None]).astype(jnp.int32), axis=1)
    cosine, sine_part = rotary_tables(own_place - before)
    key_place = jnp.arange(seq_length, dtype=jnp.int32)
    allowed = (whole_ids[None, :] == segments[:, None]) & (key_place[None, :] <= own_place[:, None])
    full_gain_attn, full_query, full_key, full_value, full_bias, full_out = (
        lax.all_gather(gain_attn, ("dp", "ctx"), axis=0, tiled=True),
        lax.all_gather(w_query, ("dp", "ctx"), axis=0, tiled=True),
        lax.all_gather(w_key, ("dp", "ctx"), axis=0, tiled=True),
        lax.all_gather(w_value, ("dp", "ctx"), axis=0, tiled=True),
        lax.all_gather(bias_qkv, ("dp", "ctx"), axis=0, tiled=True),
        lax.all_gather(w_out, ("dp", "ctx"), axis=0, tiled=True),
    )
    bias_float = full_bias.astype(jnp.float32)
    bias_query = bias_float[:width][None, :]
    bias_key = bias_float[width : width + kv_width][None, :]
    bias_value = bias_float[width + kv_width :][None, :]
    inputs = tokens.astype(jnp.float32)
    inverse_attn, normed_attn = normalize(inputs, full_gain_attn)
    normed_low = normed_attn.astype(jnp.bfloat16)
    query_rows = rotate(
        (matmul(normed_low, full_query) + bias_query).reshape(row_count, HEADS, HEAD),
        cosine,
        sine_part,
    ).astype(jnp.bfloat16)
    key_rows = (
        rotate(
            (matmul(normed_low, full_key) + bias_key).reshape(row_count, KV_HEADS, HEAD),
            cosine,
            sine_part,
        )
        .astype(jnp.bfloat16)
        .reshape(row_count, kv_width)
    )
    value_rows = (matmul(normed_low, full_value) + bias_value).astype(jnp.bfloat16)
    key_all, value_all = (
        lax.all_gather(key_rows, "ctx", axis=0, tiled=True),
        lax.all_gather(value_rows, "ctx", axis=0, tiled=True),
    )
    query_grouped = query_rows.reshape(row_count, KV_HEADS, group_width, HEAD)
    key_grouped = key_all.reshape(seq_length, KV_HEADS, HEAD)
    value_grouped = value_all.reshape(seq_length, KV_HEADS, HEAD)
    logits = attention_logits(query_grouped, key_grouped, allowed)
    row_top = jnp.max(logits, axis=-1, keepdims=True)
    weights_raw = jnp.exp(logits - row_top)
    row_total = jnp.sum(weights_raw, axis=-1, keepdims=True)
    attention_probs = weights_raw / row_total
    log_normal = row_top + jnp.log(row_total)
    mixed = jnp.einsum(
        "kgql,lkd->qkgd",
        attention_probs.astype(jnp.bfloat16),
        value_grouped,
        preferred_element_type=jnp.float32,
    )
    mixed = mixed.reshape(row_count, HEADS * HEAD).astype(jnp.bfloat16)
    hidden = inputs + matmul(mixed, full_out)
    full_gain_ffn, full_gate, full_up, full_down = (
        lax.all_gather(gain_ffn, ("dp", "ctx"), axis=0, tiled=True),
        lax.all_gather(w_gate, ("dp", "ctx"), axis=0, tiled=True),
        lax.all_gather(w_up, ("dp", "ctx"), axis=0, tiled=True),
        lax.all_gather(w_down, ("dp", "ctx"), axis=0, tiled=True),
    )
    inverse_ffn, normed_ffn = normalize(hidden, full_gain_ffn)
    ffn_low = normed_ffn.astype(jnp.bfloat16)
    gate_rows = matmul(ffn_low, full_gate)
    up_rows = matmul(ffn_low, full_up)
    sigmoid_gate = jax.nn.sigmoid(gate_rows)
    silu_gate = gate_rows * sigmoid_gate
    product = (silu_gate * up_rows).astype(jnp.bfloat16)
    output = (hidden + matmul(product, full_down)).astype(jnp.bfloat16)
    full_gain_ffn, full_gate, full_up, full_down = (
        lax.all_gather(gain_ffn, ("dp", "ctx"), axis=0, tiled=True),
        lax.all_gather(w_gate, ("dp", "ctx"), axis=0, tiled=True),
        lax.all_gather(w_up, ("dp", "ctx"), axis=0, tiled=True),
        lax.all_gather(w_down, ("dp", "ctx"), axis=0, tiled=True),
    )
    down_grad = matmul_tn(product, cotangent)
    product_grad = matmul_nt(cotangent, full_down)
    gate_grad = (
        product_grad * up_rows * sigmoid_gate * (1.0 + gate_rows * (1.0 - sigmoid_gate))
    ).astype(jnp.bfloat16)
    up_grad = (product_grad * silu_gate).astype(jnp.bfloat16)
    gate_weight_grad = matmul_tn(ffn_low, gate_grad)
    up_weight_grad = matmul_tn(ffn_low, up_grad)
    normed_ffn_grad = matmul_nt(gate_grad, full_gate) + matmul_nt(up_grad, full_up)
    gain_ffn_part, hidden_back = normalize_back(hidden, inverse_ffn, full_gain_ffn, normed_ffn_grad)
    hidden_grad = cotangent.astype(jnp.float32) + hidden_back
    grad_gain_ffn, grad_w_gate, grad_w_up, grad_w_down = (
        lax.psum_scatter(gain_ffn_part, ("dp", "ctx"), scatter_dimension=0, tiled=True),
        lax.psum_scatter(gate_weight_grad, ("dp", "ctx"), scatter_dimension=0, tiled=True),
        lax.psum_scatter(up_weight_grad, ("dp", "ctx"), scatter_dimension=0, tiled=True),
        lax.psum_scatter(down_grad, ("dp", "ctx"), scatter_dimension=0, tiled=True),
    )
    full_gain_attn, full_query, full_key, full_value, full_bias, full_out = (
        lax.all_gather(gain_attn, ("dp", "ctx"), axis=0, tiled=True),
        lax.all_gather(w_query, ("dp", "ctx"), axis=0, tiled=True),
        lax.all_gather(w_key, ("dp", "ctx"), axis=0, tiled=True),
        lax.all_gather(w_value, ("dp", "ctx"), axis=0, tiled=True),
        lax.all_gather(bias_qkv, ("dp", "ctx"), axis=0, tiled=True),
        lax.all_gather(w_out, ("dp", "ctx"), axis=0, tiled=True),
    )
    hidden_low = hidden_grad.astype(jnp.bfloat16)
    out_weight_grad = matmul_tn(mixed, hidden_low)
    mixed_grad = (
        matmul_nt(hidden_low, full_out)
        .astype(jnp.bfloat16)
        .reshape(row_count, KV_HEADS, group_width, HEAD)
    )
    logits = attention_logits(query_grouped, key_grouped, allowed)
    attention_probs = jnp.exp(logits - log_normal)
    probs_grad = jnp.einsum(
        "qkgd,lkd->kgql", mixed_grad, value_grouped, preferred_element_type=jnp.float32
    )
    value_grad_all = jnp.einsum(
        "kgql,qkgd->lkd",
        attention_probs.astype(jnp.bfloat16),
        mixed_grad,
        preferred_element_type=jnp.float32,
    )
    row_inner = jnp.sum(attention_probs * probs_grad, axis=-1, keepdims=True)
    score_grad = (attention_probs * (probs_grad - row_inner) * HEAD ** (-0.5)).astype(jnp.bfloat16)
    query_grad = jnp.einsum(
        "kgql,lkd->qkgd", score_grad, key_grouped, preferred_element_type=jnp.float32
    ).reshape(row_count, HEADS, HEAD)
    key_grad_all = jnp.einsum(
        "kgql,qkgd->lkd", score_grad, query_grouped, preferred_element_type=jnp.float32
    )
    key_grad, value_grad = (
        lax.psum_scatter(
            key_grad_all.reshape(seq_length, kv_width).astype(jnp.bfloat16),
            "ctx",
            scatter_dimension=0,
            tiled=True,
        ).astype(jnp.float32),
        lax.psum_scatter(
            value_grad_all.reshape(seq_length, kv_width).astype(jnp.bfloat16),
            "ctx",
            scatter_dimension=0,
            tiled=True,
        ).astype(jnp.float32),
    )
    query_low = (
        rotate_back(query_grad, cosine, sine_part)
        .reshape(row_count, HEADS * HEAD)
        .astype(jnp.bfloat16)
    )
    key_low = (
        rotate_back(key_grad.reshape(row_count, KV_HEADS, HEAD), cosine, sine_part)
        .reshape(row_count, kv_width)
        .astype(jnp.bfloat16)
    )
    value_low = value_grad.astype(jnp.bfloat16)
    bias_part = jnp.concatenate(
        [
            jnp.sum(query_low.astype(jnp.float32), axis=0),
            jnp.sum(key_low.astype(jnp.float32), axis=0),
            jnp.sum(value_low.astype(jnp.float32), axis=0),
        ],
        axis=0,
    )
    query_weight_grad = matmul_tn(normed_low, query_low)
    key_weight_grad = matmul_tn(normed_low, key_low)
    value_weight_grad = matmul_tn(normed_low, value_low)
    normed_attn_grad = (
        matmul_nt(query_low, full_query)
        + matmul_nt(key_low, full_key)
        + matmul_nt(value_low, full_value)
    )
    gain_attn_part, input_back = normalize_back(
        inputs, inverse_attn, full_gain_attn, normed_attn_grad
    )
    input_grad = (hidden_grad + input_back).astype(jnp.bfloat16)
    grad_gain_attn, grad_w_query, grad_w_key, grad_w_value, grad_bias_qkv, grad_w_out = (
        lax.psum_scatter(gain_attn_part, ("dp", "ctx"), scatter_dimension=0, tiled=True),
        lax.psum_scatter(query_weight_grad, ("dp", "ctx"), scatter_dimension=0, tiled=True),
        lax.psum_scatter(key_weight_grad, ("dp", "ctx"), scatter_dimension=0, tiled=True),
        lax.psum_scatter(value_weight_grad, ("dp", "ctx"), scatter_dimension=0, tiled=True),
        lax.psum_scatter(bias_part, ("dp", "ctx"), scatter_dimension=0, tiled=True),
        lax.psum_scatter(out_weight_grad, ("dp", "ctx"), scatter_dimension=0, tiled=True),
    )
    return (
        output,
        input_grad,
        grad_gain_attn,
        grad_w_query,
        grad_w_key,
        grad_w_value,
        grad_bias_qkv,
        grad_w_out,
        grad_gain_ffn,
        grad_w_gate,
        grad_w_up,
        grad_w_down,
    )


def solution(mesh):
    return jax.shard_map(
        per_device,
        mesh=mesh,
        in_specs=(
            P(("dp", "ctx"), None),
            P(("dp", "ctx")),
            P(("dp", "ctx")),
            P(("dp", "ctx"), None),
            P(("dp", "ctx"), None),
            P(("dp", "ctx"), None),
            P(("dp", "ctx")),
            P(("dp", "ctx"), None),
            P(("dp", "ctx")),
            P(("dp", "ctx"), None),
            P(("dp", "ctx"), None),
            P(("dp", "ctx"), None),
            P(("dp", "ctx"), None),
        ),
        out_specs=(
            P(("dp", "ctx"), None),
            P(("dp", "ctx"), None),
            P(("dp", "ctx")),
            P(("dp", "ctx"), None),
            P(("dp", "ctx"), None),
            P(("dp", "ctx"), None),
            P(("dp", "ctx")),
            P(("dp", "ctx"), None),
            P(("dp", "ctx")),
            P(("dp", "ctx"), None),
            P(("dp", "ctx"), None),
            P(("dp", "ctx"), None),
        ),
        check_vma=False,
    )
```

profile of v0, /device:TPU:1, one launch (start us, length us, event | category | flops | bytes accessed | tf_op | source)
XLA Modules:
  0.0 3425.3 jit_solution(13997699617278008119)
XLA Ops:
  13.2 68.9 %all-reduce.18 = (bf16[1152]{0:T(1024)(128)(2,1)S(1)}, bf16[896]{0:T(1024)(128)(2,1)S(1)}, bf16[896]{0:T(1024)(128)(2,1)S(1)}) all-reduce(bf16[1152]{0:T(1024)(128)(2,1)S(1)} %dynamic-update-slice.1, bf16[896]{0:T(1024)(128)(2,1)S(1)} %dynamic-update-slice, ...), channel_id=1, replica_groups=mesh['dp'=64,'ctx'=2] {'dp','ctx'}, use_global_device_ids=true, to_apply=%add.1 | all-reduce | flops 2944 | bytes 11776
  82.1 310.7 %all-gather.2 = bf16[128,7,128]{2,1,0:T(8,128)(2,1)S(1)} all-gather(bf16[1,7,128]{2,1,0:T(8,128)(2,1)} %bitcast.155), channel_id=1, replica_groups=mesh['dp'=64,'ctx'=2] {'dp','ctx'}, dimensions={0}, use_global_device_ids=true | all-gather | bytes 231168 | tf_op jit(solution)/shard_map/all_gather | solution.py:108
  392.9 313.5 %all-gather = bf16[128,7,128]{2,1,0:T(8,128)(2,1)S(1)} all-gather(bf16[1,7,128]{2,1,0:T(8,128)(2,1)} %bitcast.156), channel_id=1, replica_groups=mesh['dp'=64,'ctx'=2] {'dp','ctx'}, dimensions={0}, use_global_device_ids=true | all-gather | bytes 231168 | tf_op jit(solution)/shard_map/all_gather | solution.py:109
  706.9 5.2 all_gather.51
  712.2 4.6 all-gather.1
  717.5 5.1 all_gather.54
  733.7 201.7 %all-gather.18.cloned.1.call-done = bf16[128,7,4864]{2,1,0:T(8,128)(2,1)} async-done(((bf16[1,7,4864]{2,1,0:T(8,128)(2,1)}), bf16[128,7,4864]{2,1,0:T(8,128)(2,1)}) %all-gather.18.cloned.1.call-update) | async-done | bytes 8716304 | tf_op jit(solution)/shard_map/all_gather | solution.py:158
  935.4 13.5 reshape.244
  948.9 306.5 %all-gather.20.cloned.1.call-done = bf16[128,7,4864]{2,1,0:T(8,128)(2,1)} async-done(((bf16[1,7,4864]{2,1,0:T(8,128)(2,1)}), bf16[128,7,4864]{2,1,0:T(8,128)(2,1)}) %all-gather.20.cloned.1.call-update) | async-done | bytes 8716304 | tf_op jit(solution)/shard_map/all_gather | solution.py:159
  1255.4 13.5 reshape.246
  1268.9 6.6 fusion.61
  1278.4 295.0 %all-gather.22.cloned.1.call-done = bf16[128,38,896]{2,1,0:T(8,128)(2,1)} async-done(((bf16[1,38,896]{2,1,0:T(8,128)(2,1)}), bf16[128,38,896]{2,1,0:T(8,128)(2,1)}) %all-gather.22.cloned.1.call-update) | async-done | bytes 8716304 | tf_op jit(solution)/shard_map/all_gather | solution.py:160
  1573.4 13.1 reshape.248
  1586.6 8.7 multiply_convert_fusion
  1595.2 7.2 fusion.62
  1609.9 4.7 fusion.16
  1614.6 4.8 fusion.12
  1621.7 8.5 fusion.66
  1630.2 8.7 fusion.65
  1638.9 854.3 %fusion.57 = (f32[8,4864]{1,0:T(8,128)}, f32[8,4864]{1,0:T(8,128)S(1)}) fusion(f32[896,4864]{1,0:T(8,128)} %fusion.65, f32[896,4864]{1,0:T(8,128)} %fusion.66), kind=kCustom, calls=%all-reduce-scatter.3 | all-reduce-scatter fusion | flops 9961473 | bytes 35176448
  2494.8 8.5 collective-permute-start.14
  2511.6 7.4 fusion.67
  2519.0 477.4 %fusion.2 = f32[48,896]{1,0:T(8,128)} fusion(f32[4864,896]{1,0:T(8,128)} %fusion.67), kind=kCustom, calls=%all-reduce-scatter.2 | all-reduce-scatter fusion | flops 5505025 | bytes 17604608
  3004.6 5.0 collective-permute-start.31
  3014.4 7.0 collective-permute-start.12
  3024.1 11.1 collective-permute-start.10
  3045.5 5.7 collective-permute-start.6
  3057.5 4.7 collective-permute-start.3
  3066.7 4.6 collective-permute-start
  3071.3 4.6 collective-permute-start.30
  3075.8 6.3 fusion.13
  3087.6 4.8 collective-permute-start.27
  3105.2 8.8 collective-permute-start.22
  3119.8 4.1 collective-permute-start.57
  3132.3 5.0 collective-permute-start.16
  3137.7 5.4 collective-permute-start.56
  3151.3 7.2 collective-permute-start.52
  3158.7 62.9 %all-reduce.16 = (f32[896]{0:T(1024)S(1)}, f32[1152]{0:T(1024)S(1)}, f32[896]{0:T(1024)S(1)}) all-reduce(f32[896]{0:T(1024)S(1)} %get-tuple-element.14, f32[1152]{0:T(1024)S(1)} %pad_maximum_fusion.4, f32[896]{0:T(1024)S(1)} %copy-done.56), channel_id=4, replica_groups=mesh['dp'=64,'ctx'=2] {'dp','ctx'}, use_global_device_ids=true, to_apply=%region_11.12.clone | all-reduce | flops 2944 | bytes 23552
  3225.1 5.6 collective-permute-start.50
  3233.0 5.6 collective-permute-start.48
  3243.5 5.7 collective-permute-start.45
  3259.6 31.9 concatenate.29
  3294.4 7.0 collective-permute-start.40
  3304.7 7.5 collective-permute-start.38
  3315.2 30.3 concatenate.30
  3346.8 7.4 collective-permute-start.35
  3358.6 4.9 collective-permute-start.32
  3368.4 45.3 %concatenate.31 = f32[1318,896]{1,0:T(8,128)} concatenate(f32[22,896]{1,0:T(8,128)} %collective-permute-done.58, f32[48,896]{1,0:T(8,128)S(1)} %collective-permute-done.57, f32[48,896]{1,0:T(8,128)S(1)} %copy-done.25, f32[48,896]{1,0:T(8,128)S(1)} %copy-done.27, f32[48,896]{1,0:T(8,128)} %copy-done.28, f32[48,896]{1,0:T(8,128)} %copy-done.29, f32[48,896]{1,0:T(8,128)} %copy-done.30, ...), dimensions={0} | concatenate | bytes 9447424
  (321 shorter events, 163.3 us)
Async XLA Ops:
  7.2 715.5 %all-gather.14.cloned.1.call-start = ((), (), s32[]{:S(2)}) async-start(), calls=%async_computation.2 | async-start | bytes 1849344 | tf_op jit(solution)/shard_map/all_gather | solution.py:107
  7.9 718.1 %all-gather.16.cloned.1.call-start = ((), (), s32[]{:S(2)}) async-start(), calls=%async_computation.3 | async-start | bytes 1849344 | tf_op jit(solution)/shard_map/all_gather | solution.py:111
  8.7 926.7 %all-gather.18.cloned.1.call-start = ((), (), s32[]{:S(2)}) async-start(), calls=%async_computation.4 | async-start | bytes 10039296 | tf_op jit(solution)/shard_map/all_gather | solution.py:158
  9.4 1246.0 %all-gather.20.cloned.1.call-start = ((), (), s32[]{:S(2)}) async-start(), calls=%async_computation.5 | async-start | bytes 10039296 | tf_op jit(solution)/shard_map/all_gather | solution.py:159
  10.0 1563.4 %all-gather.22.cloned.1.call-start = ((), (), s32[]{:S(2)}) async-start(), calls=%async_computation.6 | async-start | bytes 9246720 | tf_op jit(solution)/shard_map/all_gather | solution.py:160
  10.6 3001.7 %reduce-scatter.13.cloned.1.call-start = ((), (), s32[]{:S(2)}) async-start(), calls=%async_computation.7 | async-start | bytes 98304
  2494.8 540.3 %collective-permute-start.14 = (f32[8,4864]{1,0:T(8,128)}, f32[8,4864]{1,0:T(8,128)}, u32[]{:S(2)}, u32[]{:S(2)}) collective-permute-start(f32[8,4864]{1,0:T(8,128)} %get-tuple-element.28), channel_id=1, source_target_pairs={{0,15},{1,16},{2,17},{3,18},{4,19},{5,20},{6,21},{7,22},{8,23},{9,... | collective-permute-start | bytes 466952
  2503.4 535.7 %collective-permute-start.13 = (f32[8,4864]{1,0:T(8,128)}, f32[8,4864]{1,0:T(8,128)}, u32[]{:S(2)}, u32[]{:S(2)}) collective-permute-start(f32[8,4864]{1,0:T(8,128)} %get-tuple-element.28), channel_id=1, source_target_pairs={{0,14},{1,15},{2,16},{3,17},{4,18},{5,19},{6,20},{7,21},{8,22},{9,... | collective-permute-start | bytes 466952
  2508.0 529.2 %reduce-scatter.15.cloned.1.call-start = ((), (), s32[]{:S(2)}) async-start(), calls=%async_computation.8 | async-start | bytes 98304
  3012.2 403.0 %all-reduce.22.cloned.1.call-start = ((), (), s32[]{:S(2)}) async-start(), calls=%async_computation.9 | async-start | bytes 14680064
  3014.4 28.2 collective-permute-start.12
  3021.4 24.1 collective-permute-start.11
  3024.1 27.2 collective-permute-start.10
  3035.2 19.8 collective-permute-start.9
  3039.0 18.5 collective-permute-start.8
  3042.7 19.5 collective-permute-start.7
  3045.5 18.6 collective-permute-start.6
  3057.5 24.7 collective-permute-start.3
  3062.2 22.0 collective-permute-start.2
  3064.2 23.4 collective-permute-start.1
  3066.7 25.8 collective-permute-start
  3071.3 24.9 collective-permute-start.30
  3084.3 19.6 collective-permute-start.28
  3092.4 21.5 collective-permute-start.26
  3096.2 19.4 collective-permute-start.25
  3100.1 19.7 collective-permute-start.24
  3103.9 20.0 collective-permute-start.23
  3105.2 22.1 collective-permute-start.22
  3119.8 31.5 collective-permute-start.57
  3137.7 85.7 %collective-permute-start.56 = (f32[48,896]{1,0:T(8,128)}, f32[48,896]{1,0:T(8,128)S(1)}, u32[]{:S(2)}, u32[]{:S(2)}) collective-permute-start(f32[48,896]{1,0:T(8,128)} %fusion.2), channel_id=1, source_target_pairs={{0,25},{1,26},{2,27},{3,28},{4,29},{5,30},{6,31},{7,32},{8,33},{9,... | collective-permute-start | bytes 516104
  3143.1 82.0 %collective-permute-start.55 = (f32[48,896]{1,0:T(8,128)}, f32[48,896]{1,0:T(8,128)S(1)}, u32[]{:S(2)}, u32[]{:S(2)}) collective-permute-start(f32[48,896]{1,0:T(8,128)} %fusion.2), channel_id=1, source_target_pairs={{0,24},{1,25},{2,26},{3,27},{4,28},{5,29},{6,30},{7,31},{8,32},{9,... | collective-permute-start | bytes 516104
  3145.1 85.6 %collective-permute-start.54 = (f32[48,896]{1,0:T(8,128)}, f32[48,896]{1,0:T(8,128)S(1)}, u32[]{:S(2)}, u32[]{:S(2)}) collective-permute-start(f32[48,896]{1,0:T(8,128)} %fusion.2), channel_id=1, source_target_pairs={{0,23},{1,24},{2,25},{3,26},{4,27},{5,28},{6,29},{7,30},{8,31},{9,... | collective-permute-start | bytes 516104
  3149.1 84.0 %collective-permute-start.53 = (f32[48,896]{1,0:T(8,128)}, f32[48,896]{1,0:T(8,128)S(1)}, u32[]{:S(2)}, u32[]{:S(2)}) collective-permute-start(f32[48,896]{1,0:T(8,128)} %fusion.2), channel_id=1, source_target_pairs={{0,22},{1,23},{2,24},{3,25},{4,26},{5,27},{6,28},{7,29},{8,30},{9,... | collective-permute-start | bytes 516104
  3151.3 87.4 %collective-permute-start.52 = (f32[48,896]{1,0:T(8,128)}, f32[48,896]{1,0:T(8,128)S(1)}, u32[]{:S(2)}, u32[]{:S(2)}) collective-permute-start(f32[48,896]{1,0:T(8,128)} %fusion.2), channel_id=1, source_target_pairs={{0,21},{1,22},{2,23},{3,24},{4,25},{5,26},{6,27},{7,28},{8,29},{9,... | collective-permute-start | bytes 516104
  3225.1 18.4 collective-permute-start.50
  3230.7 18.5 collective-permute-start.49
  3233.0 19.9 collective-permute-start.48
  3240.7 50.9 %collective-permute-start.46 = (f32[48,896]{1,0:T(8,128)}, f32[48,896]{1,0:T(8,128)}, u32[]{:S(2)}, u32[]{:S(2)}) collective-permute-start(f32[48,896]{1,0:T(8,128)} %fusion.2), channel_id=1, source_target_pairs={{0,15},{1,16},{2,17},{3,18},{4,19},{5,20},{6,21},{7,22},{8,23},{9,... | collective-permute-start | bytes 516104
  3243.5 50.9 %collective-permute-start.45 = (f32[48,896]{1,0:T(8,128)}, f32[48,896]{1,0:T(8,128)}, u32[]{:S(2)}, u32[]{:S(2)}) collective-permute-start(f32[48,896]{1,0:T(8,128)} %fusion.2), channel_id=1, source_target_pairs={{0,14},{1,15},{2,16},{3,17},{4,18},{5,19},{6,20},{7,21},{8,22},{9,... | collective-permute-start | bytes 516104
  3249.3 52.1 %collective-permute-start.44 = (f32[48,896]{1,0:T(8,128)}, f32[48,896]{1,0:T(8,128)}, u32[]{:S(2)}, u32[]{:S(2)}) collective-permute-start(f32[48,896]{1,0:T(8,128)} %fusion.2), channel_id=1, source_target_pairs={{0,13},{1,14},{2,15},{3,16},{4,17},{5,18},{6,19},{7,20},{8,21},{9,... | collective-permute-start | bytes 516104
  3252.9 51.8 %collective-permute-start.43 = (f32[48,896]{1,0:T(8,128)}, f32[48,896]{1,0:T(8,128)}, u32[]{:S(2)}, u32[]{:S(2)}) collective-permute-start(f32[48,896]{1,0:T(8,128)} %fusion.2), channel_id=1, source_target_pairs={{0,12},{1,13},{2,14},{3,15},{4,16},{5,17},{6,18},{7,19},{8,20},{9,... | collective-permute-start | bytes 516104
  3254.9 57.3 %collective-permute-start.42 = (f32[48,896]{1,0:T(8,128)}, f32[48,896]{1,0:T(8,128)}, u32[]{:S(2)}, u32[]{:S(2)}) collective-permute-start(f32[48,896]{1,0:T(8,128)} %fusion.2), channel_id=1, source_target_pairs={{0,11},{1,12},{2,13},{3,14},{4,15},{5,16},{6,17},{7,18},{8,19},{9,... | collective-permute-start | bytes 516104
  3291.6 53.9 %collective-permute-start.41 = (f32[48,896]{1,0:T(8,128)}, f32[48,896]{1,0:T(8,128)}, u32[]{:S(2)}, u32[]{:S(2)}) collective-permute-start(f32[48,896]{1,0:T(8,128)} %fusion.2), channel_id=1, source_target_pairs={{0,10},{1,11},{2,12},{3,13},{4,14},{5,15},{6,16},{7,17},{8,18},{9,... | collective-permute-start | bytes 516104
  3294.4 52.3 %collective-permute-start.40 = (f32[48,896]{1,0:T(8,128)}, f32[48,896]{1,0:T(8,128)}, u32[]{:S(2)}, u32[]{:S(2)}) collective-permute-start(f32[48,896]{1,0:T(8,128)} %fusion.2), channel_id=1, source_target_pairs={{0,9},{1,10},{2,11},{3,12},{4,13},{5,14},{6,15},{7,16},{8,17},{9,1... | collective-permute-start | bytes 516104
  3301.4 52.7 %collective-permute-start.39 = (f32[48,896]{1,0:T(8,128)}, f32[48,896]{1,0:T(8,128)}, u32[]{:S(2)}, u32[]{:S(2)}) collective-permute-start(f32[48,896]{1,0:T(8,128)} %fusion.2), channel_id=1, source_target_pairs={{0,8},{1,9},{2,10},{3,11},{4,12},{5,13},{6,14},{7,15},{8,16},{9,17... | collective-permute-start | bytes 516104
  3304.7 51.4 %collective-permute-start.38 = (f32[48,896]{1,0:T(8,128)}, f32[48,896]{1,0:T(8,128)}, u32[]{:S(2)}, u32[]{:S(2)}) collective-permute-start(f32[48,896]{1,0:T(8,128)} %fusion.2), channel_id=1, source_target_pairs={{0,7},{1,8},{2,9},{3,10},{4,11},{5,12},{6,13},{7,14},{8,15},{9,16}... | collective-permute-start | bytes 516104
  3312.2 46.4 %collective-permute-start.37 = (f32[48,896]{1,0:T(8,128)}, f32[48,896]{1,0:T(8,128)}, u32[]{:S(2)}, u32[]{:S(2)}) collective-permute-start(f32[48,896]{1,0:T(8,128)} %fusion.2), channel_id=1, source_target_pairs={{0,6},{1,7},{2,8},{3,9},{4,10},{5,11},{6,12},{7,13},{8,14},{9,15},... | collective-permute-start | bytes 516104
  3345.5 18.7 collective-permute-start.36
  (81 other events, 9706.1 us)
Sparse Core Ops, SparseCore 0:
  9.7 303.9 all-gather.13
  315.4 299.8 all-gather.15
  617.0 318.3 all-gather.17
  937.0 318.3 all-gather.19
  1256.9 316.4 all-gather.21
  2508.1 13.9 reduce-scatter.12
  3012.4 17.7 reduce-scatter.14
  3039.1 234.4 all-reduce.21
where the time goes:
time: 3440 us; the launch traced here: 3430 us
  blocking collectives  2100 us (61%)
  waiting for transfers between devices  811 us (24%)
  starting transfers between devices  231 us (7%)
  local copies, waits for them, and re-layouts  172 us (5%)
  matrix products  85.7 us (2%)
    unnamed x4, blocking collectives  1460 us
    all_gather x1, blocking collectives, per_device(): lax.all_gather(w_value, ('dp', 'ctx'), axis=0, tiled=True)  313 us
    all_gather x1, blocking collectives, per_device(): lax.all_gather(w_key, ('dp', 'ctx'), axis=0, tiled=True)  311 us
    all_gather x1, waiting for transfers between devices, per_device(): lax.all_gather(w_up, ('dp', 'ctx'), axis=0, tiled=True)  306 us
    all_gather x1, waiting for transfers between devices, per_device(): lax.all_gather(w_down, ('dp', 'ctx'), axis=0, tiled=True)  295 us
    unnamed x62, starting transfers between devices  231 us
    all_gather x1, waiting for transfers between devices, per_device(): lax.all_gather(w_gate, ('dp', 'ctx'), axis=0, tiled=True)  202 us
    unnamed x155, local copies, waits for them, and re-layouts  172 us
  transfers between devices with their start and end apart: 67, of which 5 were waited for; matrix products, arithmetic and copies ran while one was open for 20% of the time, Pallas kernels for 0%

commit v1 on v0

v1 whole, which is shorter than its diff:
```python
import functools

import jax
import jax.numpy as jnp
import numpy as np
from jax import lax
from jax.experimental import pallas as pl
from jax.experimental.pallas import tpu as pltpu
from jax.sharding import PartitionSpec as P

F32 = jnp.float32
BF16 = jnp.bfloat16
MESH = pl.DeviceIdType.MESH
D = 896
DP = 1024
FF = 4864
FS = 640
T = 128
VEC = 2 * D + 1152
EPS = 1e-6
MASKED = -1e9
ORDERS = (("x", "z", "y"), ("z", "x", "y"), ("y", "x", "z"), ("y", "z", "x"))


def iota(shape, axis):
    return lax.broadcasted_iota(jnp.int32, shape, axis)


def sevenths(v):
    return lax.shift_right_logical(v * 9363, 16)


def ninths(v):
    return lax.shift_right_logical(v * 7282, 16)


def slot_of(i):
    return (i >> 5) * 32 + ((i >> 2) & 3) * 8 + (i & 1) * 4 + ((i >> 4) & 1) * 2 + ((i >> 1) & 1)


def one_hot(test):
    return jnp.where(test, 1.0, 0.0).astype(BF16)


def mm(a, b):
    return jnp.dot(a, b, preferred_element_type=F32)


def mm_nt(a, b):
    return lax.dot_general(a, b, (((1,), (1,)), ((), ())), preferred_element_type=F32)


def mm_tn(a, b):
    return lax.dot_general(a, b, (((0,), (0,)), ((), ())), preferred_element_type=F32)


def split(v):
    hi = v.astype(BF16)
    return hi, (v - hi.astype(F32)).astype(BF16)


SCRATCH = dict(
    pkf=((8, 2048), F32),
    pk=((4, 16, 256), BF16),
    pkr=((4, 16, 256), BF16),
    aw=((8, 4, 4, 4, 16, 256), BF16),
    guf=((2, 8, 8, FS), F32),
    gus=((8, 16, FS), BF16),
    gui=((8, 16, FS), BF16),
    wg=((4, 4, 64, FS), BF16),
    wu=((4, 4, 64, FS), BF16),
    da=((4, 4, 40, 512), BF16),
    db=((4, 4, 40, 384), BF16),
    pad=((D, DP), BF16),
    order=((FS, FS), BF16),
    pick=((32, VEC), BF16),
    mask=((128, VEC), BF16),
    wdf=((40, D), F32),
    segs=((2, 8, 128), jnp.int32),
    kv=((2, T, 256), BF16),
    prob=((14, T, 256), F32),
    ball=((4, 2, T, DP), BF16),
    yall=((4, 2, T, D), BF16),
    mb=((4, 2 * T, FS), BF16),
    dgb=((4, 2 * T, FS), BF16),
    dub=((4, 2 * T, FS), BF16),
    po=((4, 2, T, D), BF16),
    pd=((4, 2, T, DP), BF16),
    qo=((4, T, D), BF16),
    qd=((4, T, DP), BF16),
    ro=((3, T, D), BF16),
    rd=((3, T, DP), BF16),
    gg=((4, 4, 64, FS), BF16),
    gu=((4, 4, 64, FS), BF16),
    ga=((4, 4, 40, 512), BF16),
    gb=((4, 4, 40, 384), BF16),
    rg1=((3, 4, 64, FS), BF16),
    ru1=((3, 4, 64, FS), BF16),
    ra1=((3, 4, 40, 512), BF16),
    rb1=((3, 4, 40, 384), BF16),
    sg1=((4, 64, FS), BF16),
    su1=((4, 64, FS), BF16),
    sa1=((4, 40, 512), BF16),
    sb1=((4, 40, 384), BF16),
    rg2=((3, 64, FS), BF16),
    ru2=((3, 64, FS), BF16),
    ra2=((3, 40, 512), BF16),
    rb2=((3, 40, 384), BF16),
    fs=((8, 2, 8, FS), F32),
    fr=((8, 2, 8, FS), F32),
    dkv=((2, T, 256), BF16),
    dkvf=((2, T, 256), F32),
    dkr=((T, 256), BF16),
    gat=((8, 4, 4, 4, 16, 256), BF16),
    gar=((4, 4, 4, 4, 16, 256), BF16),
    r1=((4, 3, 4, 4, 16, 256), BF16),
    t2=((4, 4, 4, 16, 256), BF16),
    r2=((4, 3, 4, 16, 256), BF16),
    t3=((4, 4, 16, 256), BF16),
    r3=((4, 3, 16, 256), BF16),
    fin=((4, 16, 256), F32),
    finr=((4, 8, 256), F32),
)
NSEM = 200


def body(tok, seg, gain_attn, wq, wk, wv, bias_qkv, wo, gain_ffn, wgate, wup, wdown, cot,
         out, ing, g_gain_attn, g_wq, g_wk, g_wv, g_bias, g_wo, g_gain_ffn, g_gate, g_up, g_down, *rest):
    s = dict(zip(SCRATCH, rest))
    ssem, rsem = rest[len(SCRATCH):]
    count = [0]
    sends = []
    di, yh = lax.axis_index("dp"), lax.axis_index("ctx")
    c, z, yl, x = di % 2, (di // 2) % 4, (di // 8) % 2, di // 16
    y = yh * 2 + yl
    here = {"x": x, "y": y, "z": z}

    def device(x, y, z, c):
        return (((x * 2 + y % 2) * 4 + z) * 2 + c, y // 2)

    def along(axis, k):
        at = dict(here)
        at[axis] = (at[axis] + k) % 4
        return device(at["x"], at["y"], at["z"], c)

    sibling = device(x, y, z, 1 - c)

    def remote(src, dst, dev):
        n = count[0]
        count[0] += 1
        copy = pltpu.make_async_remote_copy(
            src_ref=src, dst_ref=dst, send_sem=ssem.at[n], recv_sem=rsem.at[n],
            device_id=dev, device_id_type=MESH)
        copy.start()
        sends.append(copy)
        return copy

    def landed(copies):
        for copy in copies:
            copy.wait_recv()

    barrier = pltpu.get_barrier_semaphore()
    partners = [along(axis, k) for axis in "xyz" for k in (1, 2, 3)] + [sibling]
    partners += [device(x, (y + k) % 4, z, 1 - c) for k in (1, 2, 3)]
    for dev in partners:
        pl.semaphore_signal(barrier, inc=1, device_id=dev, device_id_type=MESH)

    pkf = s["pkf"]
    pkf[0:7, 0:896] = wq[...].astype(F32)
    pkf[0:7, 896:1024] = wk[...].astype(F32)
    pkf[0:7, 1024:1152] = wv[...].astype(F32)
    pkf[0:7, 1152:2048] = wo[...].astype(F32)
    pkf[7:8, :] = jnp.zeros((1, 2048), F32)
    pkf[7:8, 0:7] = gain_attn[...].astype(F32)
    pkf[7:8, 7:14] = gain_ffn[...].astype(F32)
    pkf[7:8, 14:23] = bias_qkv[...].astype(F32)
    for p in range(4):
        s["pk"][p] = jnp.concatenate(
            [pkf[:, 256 * p:256 * p + 256], pkf[:, 1024 + 256 * p:1280 + 256 * p]], axis=0).astype(BF16)
    s["segs"][yh] = jnp.broadcast_to(seg[...], (8, 128))
    s["yall"][y, c] = cot[...]

    pad, order, pick, mask = s["pad"], s["order"], s["pick"], s["mask"]
    r = iota((FS, 1), 0)
    u = lax.shift_right_logical(r * 1725, 16)
    target = (u & 3) * 160 + (u >> 2) * 40 + (r - u * 38)
    order[...] = one_hot((iota((FS, FS), 1) == target) & (r < 608))

    pl.semaphore_wait(barrier, len(partners))
    swap = remote(s["pk"], s["pkr"], sibling)
    seg_copy = remote(s["segs"].at[yh], s["segs"].at[yh], along("y", 2))

    guf = s["guf"]
    guf[...] = jnp.zeros(guf.shape, F32)
    for k in range(8):
        guf[0, k, 0:7, 0:608] = wgate[:, 608 * k:608 * k + 608].astype(F32)
        guf[1, k, 0:7, 0:608] = wup[:, 608 * k:608 * k + 608].astype(F32)
    placed = mm(guf[...].reshape(128, FS).astype(BF16), order[...]).reshape(2, 4, 2, 8, FS)
    lane = iota((32, FS), 1)
    for q in range(4):
        piece = jnp.zeros((32, FS), F32)
        for xx in range(4):
            moved = placed[:, xx].reshape(32, FS)
            if xx != q:
                moved = pltpu.roll(moved, (160 * (xx - q)) % FS, 1)
            piece = jnp.where((lane >= 160 * xx) & (lane < 160 * xx + 160), moved, piece)
        piece = piece.reshape(2, 2, 8, FS)
        for yy in range(2):
            s["gus"][(2 * (q % 2) + yy) * 2 + q // 2] = jnp.concatenate(
                [piece[0, yy], piece[1, yy]], axis=0).astype(BF16)
    me8 = y * 2 + c
    gu_in = []
    for k in range(4):
        for e in range(2):
            if k or e:
                ty, tc = (y + k) % 4, (c + e) % 2
                gu_in.append(remote(s["gus"].at[ty * 2 + tc], s["gui"].at[me8], device(x, ty, z, tc)))
    s["gui"][me8] = s["gus"][me8]

    swap.wait_recv()
    for p in range(4):
        own, other = s["pk"][p].astype(F32), s["pkr"][p].astype(F32)
        first = jnp.concatenate([own[0:8], other[0:8]], axis=0)
        second = jnp.concatenate([other[8:16], own[8:16]], axis=0)
        s["aw"][4 * c + p, x, z, y] = jnp.where(c == 0, first, second).astype(BF16)

    def region(ref, axes):
        at = [here[a] if a not in axes else slice(None) for a in "xzy"]
        return ref.at[tuple(at)]

    def attn_phase(phase):
        copies = []
        for p, axes in enumerate(ORDERS):
            part = region(s["aw"].at[4 * c + p], axes[:phase])
            copies.append([remote(part, part, along(axes[phase], k)) for k in (1, 2, 3)])
        return copies

    first = attn_phase(0)

    wdf = s["wdf"]
    wdf[0:38] = wdown[...].astype(F32)
    wdf[38:40] = jnp.zeros((2, D), F32)
    s["da"][x, z] = wdf[:, 0:512].astype(BF16)
    s["db"][x, z] = wdf[:, 512:896].astype(BF16)
    landed(gu_in)
    for yy in range(4):
        even, odd = s["gui"][2 * yy].astype(F32), s["gui"][2 * yy + 1].astype(F32)
        rows = pl.ds(16 * yy, 16)
        s["wg"][x, z, rows] = jnp.concatenate([even[0:8], odd[0:8]], axis=0).astype(BF16)
        s["wu"][x, z, rows] = jnp.concatenate([even[8:16], odd[8:16]], axis=0).astype(BF16)

    def ffn_phase(phase):
        copies = []
        for name, axes in (("wg", "xz"), ("wu", "zx"), ("da", "xz"), ("db", "zx")):
            at = [here[a] if a not in axes[:phase] else slice(None) for a in "xz"]
            part = s[name].at[tuple(at)]
            copies += [remote(part, part, along(axes[phase], k)) for k in (1, 2, 3)]
        return copies

    ffn1 = ffn_phase(0)
    for at in range(0, D, 128):
        d = iota((128, 1), 0) + at
        i = sevenths(d)
        pad[at:at + 128] = one_hot(iota((128, DP), 1) == slot_of(i) * 8 + (d - i * 7))
    for group in first:
        landed(group)
    second = attn_phase(1)
    landed(ffn1)
    ffn2 = ffn_phase(1)
    for group in second:
        landed(group)
    third = attn_phase(2)

    ymine = s["yall"].at[y, c]
    y_sib = remote(ymine, ymine, sibling)
    y_ring = [remote(ymine, ymine, along("y", k)) for k in (1, 2, 3)]

    xf = tok[...].astype(F32)
    r1 = lax.rsqrt(jnp.mean(xf * xf, axis=-1, keepdims=True) + EPS)
    seg_copy.wait_recv()
    rows0 = s["segs"][0][0:1].astype(F32)
    rows1 = s["segs"][1][0:1].astype(F32)
    own_row = jnp.where(yh == 0, rows0, rows1)
    diag = iota((T, T), 0) == iota((T, T), 1)
    own_seg = jnp.sum(jnp.where(diag, own_row, 0.0), axis=1, keepdims=True)
    length = jnp.sum(2.0 * T - jnp.sum(rows0 + rows1, axis=1, keepdims=True), axis=0, keepdims=True)
    base = (yh * T).astype(F32)
    place = iota((T, 128), 0).astype(F32) + base
    lane128 = iota((T, 128), 1)
    expo = (lane128 % 32).astype(F32) * (-2.0 / 64.0)
    freq = jnp.exp(expo * float(np.log(1e6)))
    angle = (place - own_seg * length) * freq
    cosine = jnp.cos(angle)
    low_half = lane128 % 64 < 32
    sine = jnp.where(low_half, -jnp.sin(angle), jnp.sin(angle))

    def swapped(v):
        return jnp.where(low_half, pltpu.roll(v, 96, 1), pltpu.roll(v, 32, 1))

    key_seg = jnp.concatenate([rows0, rows1], axis=1)
    key_at = iota((T, 256), 1)
    query_at = iota((T, 256), 0) + yh * T
    allowed = (key_seg == own_seg) & (key_at <= query_at)
    last_rows = one_hot(iota((128, DP), 1) == iota((128, DP), 0) * 8 + 7)
    n = iota((1, VEC), 1)
    d = jnp.where(n >= D, n - D, n)
    i = sevenths(d)
    m = n - 2 * D
    im = ninths(m)
    lane_of = jnp.where(m >= 0, 14 + m - im * 9, d - i * 7 + jnp.where(n >= D, 7, 0))
    pick[...] = one_hot(iota((32, VEC), 0) == lane_of)
    mask[...] = one_hot(iota((128, VEC), 0) == slot_of(jnp.where(m >= 0, im, i)))

    forward = []
    for p, axes in enumerate(ORDERS):
        part = region(s["aw"].at[4 * c + p], axes[:2])
        forward.append(remote(part, part, sibling))
    for k in (1, 2, 3):
        for p, axes in enumerate(ORDERS):
            third[p][k - 1].wait_recv()
            at = [slice(None)] * 3
            at["xzy".index(axes[2])] = (here[axes[2]] - k) % 4
            part = s["aw"].at[4 * c + p].at[tuple(at)]
            forward.append(remote(part, part, sibling))
    landed(forward)

    def weight(g):
        return s["aw"][g].reshape(DP, 256)

    picked = mm(last_rows, weight(0)[:, 0:128])[:, 0:32].astype(BF16)
    vecs = jnp.sum(mm(picked, pick[...]) * mask[...].astype(F32), axis=0, keepdims=True)
    gain_a, gain_f, bias = vecs[:, 0:D], vecs[:, D:2 * D], vecs[:, 2 * D:]

    a = (xf * r1 * gain_a).astype(BF16)
    a_pad = mm(a, pad[...]).astype(BF16)
    qkv = [mm(a_pad, weight(g)) for g in range(4)]
    qkv.append(mm(a_pad, weight(4)[:, 0:128]))

    def tile(t):
        v = qkv[t // 2] if t == 8 else qkv[t // 2][:, 128 * (t % 2):128 * (t % 2) + 128]
        return v + bias[:, 128 * t:128 * t + 128]

    def rope(v):
        return v * cosine + swapped(v) * sine

    key_tile = rope(tile(7)).astype(BF16)
    value_tile = tile(8).astype(BF16)
    s["kv"][yh] = jnp.concatenate([key_tile, value_tile], axis=1)
    kv_copy = remote(s["kv"].at[yh], s["kv"].at[yh], along("y", 2))
    q_tiles = [rope(tile(t)).astype(BF16) for t in range(7)]

    y_fwd = []
    for k in (1, 2, 3):
        y_ring[k - 1].wait_recv()
        part = s["yall"].at[(y - k) % 4, c]
        y_fwd.append(remote(part, part, sibling))

    kv_copy.wait_recv()
    kv = s["kv"][...].reshape(256, 256).astype(F32)
    lane256 = iota((256, 128), 1)

    def halves(v):
        turned = pltpu.roll(v, 64, 1)
        lo, hi = lane256 < 64, lane256 >= 64
        pick2 = lambda m, u: jnp.where(m, u, 0.0).astype(BF16)
        return ((pick2(lo, v), pick2(hi, turned)), (pick2(lo, turned), pick2(hi, v)))

    keys = halves(kv[:, 0:128])
    values = halves(kv[:, 128:256])
    mixed = []
    for t in range(7):
        total = None
        for e in range(2):
            h = 2 * t + e
            logits = jnp.where(allowed, mm_nt(q_tiles[t], keys[h // 7][e]) * 0.125, MASKED)
            top = jnp.max(logits, axis=-1, keepdims=True)
            raw = jnp.exp(logits - top)
            pr = raw / jnp.sum(raw, axis=-1, keepdims=True)
            s["prob"][h] = pr
            part = mm(pr.astype(BF16), values[h // 7][e])
            total = part if total is None else total + part
        mixed.append(total.astype(BF16))
    mixed = jnp.concatenate(mixed, axis=1)
    o_pad = mm(mixed, pad[...]).astype(BF16)
    att = jnp.concatenate(
        [mm(o_pad, weight(4)[:, 128:256])] + [mm(o_pad, weight(g)) for g in (5, 6, 7)], axis=1)
    hidden = xf + att
    r2 = lax.rsqrt(jnp.mean(hidden * hidden, axis=-1, keepdims=True) + EPS)
    b = (hidden * r2 * gain_f).astype(BF16)
    s["ball"][y, c] = mm(b, pad[...]).astype(BF16)
    bmine = s["ball"].at[y, c]
    b_sib = remote(bmine, bmine, sibling)
    b_ring = [remote(bmine, bmine, along("y", k)) for k in (1, 2, 3)]

    landed(ffn2)
    b_fwd = []
    for k in (1, 2, 3):
        b_ring[k - 1].wait_recv()
        part = s["ball"].at[(y - k) % 4, c]
        b_fwd.append(remote(part, part, sibling))
    landed([y_sib, b_sib] + y_fwd)

    base = count[0]
    count[0] += 16

    def chunk_copies(k):
        yy = (y + k) % 4
        copies = []
        for j, (part, got, ring) in enumerate((("pd", "qd", "rd"), ("po", "qo", "ro"))):
            n = base + 8 * j + k
            copies.append(pltpu.make_async_remote_copy(
                src_ref=s[part].at[yy, 1 - c], dst_ref=s[got].at[yy], send_sem=ssem.at[n], recv_sem=rsem.at[n],
                device_id=sibling, device_id_type=MESH))
            copies.append(pltpu.make_async_remote_copy(
                src_ref=s[part].at[yy, c], dst_ref=s[ring].at[k - 1], send_sem=ssem.at[n + 4],
                recv_sem=rsem.at[n + 4], device_id=along("y", k), device_id_type=MESH))
        return copies

    def chunk(step, carry):
        k = 3 - step
        d_sib, d_ring, o_sib, o_ring = chunk_copies(k)
        yy = (y + k) % 4
        bt = s["ball"][yy].reshape(2 * T, DP)
        yt = s["yall"][yy].reshape(2 * T, D)
        gate_w, up_w = s["wg"][...].reshape(DP, FS), s["wu"][...].reshape(DP, FS)
        down_a, down_b = s["da"][...].reshape(FS, 512), s["db"][...].reshape(FS, 384)
        gate, up = mm(bt, gate_w), mm(bt, up_w)
        sg = 1.0 / (1.0 + jnp.exp(-gate))
        silu = gate * sg
        m = (silu * up).astype(BF16)
        dm = mm_nt(yt[:, 0:512], down_a) + mm_nt(yt[:, 512:896], down_b)
        dgate = (dm * up * sg * (1.0 + gate * (1.0 - sg))).astype(BF16)
        dup = (dm * silu).astype(BF16)
        s["mb"][yy], s["dgb"][yy], s["dub"][yy] = m, dgate, dup
        s["pd"][yy] = (mm_nt(dgate, gate_w) + mm_nt(dup, up_w)).astype(BF16).reshape(2, T, DP)
        d_sib.start()
        s["po"][yy, :, :, 0:512] = mm(m, down_a).astype(BF16).reshape(2, T, 512)
        s["po"][yy, :, :, 512:896] = mm(m, down_b).astype(BF16).reshape(2, T, 384)
        o_sib.start()
        d_sib.wait_recv()
        s["pd"][yy, c] = (s["pd"][yy, c].astype(F32) + s["qd"][yy].astype(F32)).astype(BF16)

        @pl.when(k > 0)
        def _():
            d_ring.start()

        o_sib.wait_recv()
        s["po"][yy, c] = (s["po"][yy, c].astype(F32) + s["qo"][yy].astype(F32)).astype(BF16)

        @pl.when(k > 0)
        def _():
            o_ring.start()

        return carry

    landed(b_fwd)
    lax.fori_loop(0, 4, chunk, 0)
    red_d, red_o = [], []
    for k in range(4):
        d_sib, d_ring, o_sib, o_ring = chunk_copies(k)
        sends.extend([d_sib, o_sib])
        if k:
            sends.extend([d_ring, o_ring])
            red_d.append(d_ring)
            red_o.append(o_ring)

    ball = s["ball"][...].reshape(1024, DP)
    s["gg"][...] = mm_tn(ball, s["dgb"][...].reshape(1024, FS)).astype(BF16).reshape(4, 4, 64, FS)
    s["gu"][...] = mm_tn(ball, s["dub"][...].reshape(1024, FS)).astype(BF16).reshape(4, 4, 64, FS)
    down = mm_tn(s["mb"][...].reshape(1024, FS), s["yall"][...].reshape(1024, D))
    s["ga"][...] = down[:, 0:512].reshape(4, 4, 40, 512).astype(BF16)
    s["gb"][...] = down[:, 512:896].reshape(4, 4, 40, 384).astype(BF16)
    FG = (("gg", "rg1", "sg1", "rg2", "zx"), ("gu", "ru1", "su1", "ru2", "xz"),
          ("ga", "ra1", "sa1", "ra2", "zx"), ("gb", "rb1", "sb1", "rb2", "xz"))

    def plane(ref, axis, index):
        return ref.at[index] if axis == "x" else ref.at[:, index]

    fg1 = []
    for src, r_1, s_1, r_2, axes in FG:
        for k in (1, 2, 3):
            there = (here[axes[0]] + k) % 4
            fg1.append(remote(plane(s[src], axes[0], there), s[r_1].at[k - 1], along(axes[0], k)))

    landed(red_d)
    db_pad = s["pd"][y, c].astype(F32)
    for k in (1, 2, 3):
        db_pad = db_pad + s["rd"][k - 1].astype(F32)
    hi, lo = split(db_pad)
    dbv = mm_nt(hi, pad[...]) + mm_nt(lo, pad[...])
    gain_f_grad = jnp.sum(dbv * hidden * r2, axis=0, keepdims=True)
    ev = dbv * gain_f
    inner = jnp.mean(ev * hidden, axis=-1, keepdims=True)
    dh = cot[...].astype(F32) + r2 * ev - hidden * (r2 * r2 * r2 * inner)
    dh_low = dh.astype(BF16)
    do_pad = mm_nt(dh_low[:, 0:128], weight(4)[:, 128:256])
    for g in (5, 6, 7):
        at = 128 + 256 * (g - 5)
        do_pad = do_pad + mm_nt(dh_low[:, at:at + 256], weight(g))
    do = mm_nt(do_pad.astype(BF16), pad[...]).astype(BF16)

    dk = [[None, None], [None, None]]
    dv = [[None, None], [None, None]]
    dq_tiles = []
    for t in range(7):
        do_t = do[:, 128 * t:128 * t + 128]
        total = None
        for e in range(2):
            h = 2 * t + e
            g = h // 7
            pr = s["prob"][h]
            dpr = mm_nt(do_t, values[g][e])
            ds = (pr * (dpr - jnp.sum(pr * dpr, axis=-1, keepdims=True)) * 0.125).astype(BF16)
            part = mm(ds, keys[g][e])
            total = part if total is None else total + part
            kp, vp = mm_tn(ds, q_tiles[t]), mm_tn(pr.astype(BF16), do_t)
            dk[g][e] = kp if dk[g][e] is None else dk[g][e] + kp
            dv[g][e] = vp if dv[g][e] is None else dv[g][e] + vp
        dq_tiles.append((total * cosine - swapped(total) * sine).astype(BF16))

    def gather(parts):
        lo = parts[0][0] + pltpu.roll(parts[0][1], 64, 1)
        hi = parts[1][1] + pltpu.roll(parts[1][0], 64, 1)
        return jnp.where(lane256 < 64, lo, hi)

    dkv = jnp.concatenate([gather(dk), gather(dv)], axis=1).reshape(2, T, 256)
    s["dkvf"][...] = dkv
    s["dkv"][...] = dkv.astype(BF16)
    dkv_copy = remote(s["dkv"].at[1 - yh], s["dkr"], along("y", 2))

    landed(red_o)
    total = hidden + s["po"][y, c].astype(F32)
    for k in (1, 2, 3):
        total = total + s["ro"][k - 1].astype(F32)
    out[...] = total.astype(BF16)

    def grad(g, value):
        s["gat"][g] = value.astype(BF16).reshape(4, 4, 4, 16, 256)

    out_grad = mm_tn(o_pad, dh_low)
    for g in (5, 6, 7):
        at = 128 + 256 * (g - 5)
        grad(g, out_grad[:, at:at + 256])
    dq = jnp.concatenate(dq_tiles, axis=1)
    dkv_copy.wait_recv()
    dkv_own = s["dkvf"][yh] + s["dkr"][...].astype(F32)
    dko, dvl = dkv_own[:, 0:128], dkv_own[:, 128:256].astype(BF16)
    dkl = (dko * cosine - swapped(dko) * sine).astype(BF16)
    dqkv = jnp.concatenate([dq, dkl, dvl], axis=1)
    da_pad = mm_nt(dqkv[:, 1024:1152], weight(4)[:, 0:128])
    for g in range(4):
        da_pad = da_pad + mm_nt(dqkv[:, 256 * g:256 * g + 256], weight(g))
    hi, lo = split(da_pad)
    dav = mm_nt(hi, pad[...]) + mm_nt(lo, pad[...])
    gain_a_grad = jnp.sum(dav * xf * r1, axis=0, keepdims=True)
    bias_grad = jnp.sum(dqkv.astype(F32), axis=0, keepdims=True)
    small = jnp.concatenate([gain_a_grad, gain_f_grad, bias_grad], axis=1)
    spread = (mask[...].astype(F32) * small).astype(BF16)
    small_rows = mm_nt(spread, pick[...]).astype(BF16)
    small_rows = mm_tn(last_rows, jnp.concatenate([small_rows, jnp.zeros((128, 96), BF16)], axis=1))
    for g in range(4):
        value = mm_tn(a_pad, dqkv[:, 256 * g:256 * g + 256])
        if g == 0:
            value = jnp.concatenate([value[:, 0:128] + small_rows, value[:, 128:256]], axis=1)
        grad(g, value)
    grad(4, jnp.concatenate([mm_tn(a_pad, dvl), out_grad[:, 0:128]], axis=1))
    gat_copy = remote(s["gat"].at[pl.ds((1 - c) * 4, 4)], s["gar"], sibling)

    fv = dav * gain_a
    inner = jnp.mean(fv * xf, axis=-1, keepdims=True)
    ing[...] = (dh + r1 * fv - xf * (r1 * r1 * r1 * inner)).astype(BF16)

    gat_copy.wait_recv()
    for p in range(4):
        s["gat"][4 * c + p] = (s["gat"][4 * c + p].astype(F32) + s["gar"][p].astype(F32)).astype(BF16)

    def cut(axes, axis, index):
        order3 = [a for a in "xzy" if a in axes]
        at = [slice(None)] * len(order3)
        at[order3.index(axis)] = index
        return tuple(at)

    def reduce_phase(src, dst, phase):
        copies = []
        for p, axes in enumerate(ORDERS):
            left, axis = axes[:3 - phase], axes[2 - phase]
            for k in (1, 2, 3):
                there = (here[axis] + k) % 4
                part = s[src].at[4 * c + p if src == "gat" else p].at[cut(left, axis, there)]
                copies.append(remote(part, s[dst].at[p, k - 1], along(axis, k)))
        return copies

    def reduce_sum(src, dst, phase):
        sums = []
        for p, axes in enumerate(ORDERS):
            left, axis = axes[:3 - phase], axes[2 - phase]
            total = s[src][(4 * c + p if src == "gat" else p,) + cut(left, axis, here[axis])].astype(F32)
            for k in (1, 2, 3):
                total = total + s[dst][p, k - 1].astype(F32)
            sums.append(total)
        return sums

    ph1 = reduce_phase("gat", "r1", 0)

    landed(fg1)
    fg2 = []
    for src, r_1, s_1, r_2, axes in FG:
        own = s[src][here["x"]] if axes[0] == "x" else s[src][:, here["z"]]
        total = own.astype(F32)
        for k in (1, 2, 3):
            total = total + s[r_1][k - 1].astype(F32)
        s[s_1][...] = total.astype(BF16)
        for k in (1, 2, 3):
            there = (here[axes[1]] + k) % 4
            fg2.append(remote(s[s_1].at[there], s[r_2].at[k - 1], along(axes[1], k)))

    landed(ph1)
    for p, total in enumerate(reduce_sum("gat", "r1", 0)):
        s["t2"][p] = total.astype(BF16)
    ph2 = reduce_phase("t2", "r2", 1)

    landed(fg2)
    sums = []
    for src, r_1, s_1, r_2, axes in FG:
        total = s[s_1][here[axes[1]]].astype(F32)
        for k in (1, 2, 3):
            total = total + s[r_2][k - 1].astype(F32)
        sums.append(total)
    g_down[:, 0:512] = sums[2][0:38]
    g_down[:, 512:896] = sums[3][0:38]
    s["fs"][:, 0] = sums[0].reshape(8, 8, FS)
    s["fs"][:, 1] = sums[1].reshape(8, 8, FS)
    fin_in = []
    for k in range(4):
        for e in range(2):
            if k or e:
                ty, tc = (y + k) % 4, (c + e) % 2
                fin_in.append(remote(s["fs"].at[ty * 2 + tc], s["fr"].at[me8], device(x, ty, z, tc)))
    s["fr"][me8] = s["fs"][me8]

    landed(ph2)
    for p, total in enumerate(reduce_sum("t2", "r2", 1)):
        s["t3"][p] = total.astype(BF16)
    ph3 = reduce_phase("t3", "r3", 2)

    landed(fin_in)
    for yy in range(2):
        for xx in range(4):
            block = jnp.zeros((16, FS), F32)
            lane16 = iota((16, FS), 1)
            for q in range(4):
                moved = s["fr"][(2 * (q % 2) + yy) * 2 + q // 2].reshape(16, FS)
                if xx != q:
                    moved = pltpu.roll(moved, (160 * (q - xx)) % FS, 1)
                block = jnp.where((lane16 >= 160 * q) & (lane16 < 160 * q + 160), moved, block)
            guf[:, 2 * xx + yy] = block.reshape(2, 8, FS)
    hi, lo = split(guf[...].reshape(128, FS))
    flat = (mm_nt(hi, order[...]) + mm_nt(lo, order[...])).reshape(2, 8, 8, FS)
    for g, ref in enumerate((g_gate, g_up)):
        for k in range(8):
            ref[:, 608 * k:608 * k + 608] = flat[g, k, 0:7, 0:608]

    landed(ph3)
    for p, total in enumerate(reduce_sum("t3", "r3", 2)):
        s["fin"][p] = total
    fin_copy = remote(s["fin"].at[:, pl.ds((1 - c) * 8, 8)], s["finr"], sibling)
    fin_copy.wait_recv()
    for p in range(4):
        own = jnp.where(c == 0, s["fin"][p, 0:8], s["fin"][p, 8:16])
        other = s["finr"][p]
        pkf[:, 256 * p:256 * p + 256] = jnp.where(c == 0, own, other)
        pkf[:, 1024 + 256 * p:1280 + 256 * p] = jnp.where(c == 0, other, own)
    g_wq[...] = pkf[0:7, 0:896]
    g_wk[...] = pkf[0:7, 896:1024]
    g_wv[...] = pkf[0:7, 1024:1152]
    g_wo[...] = pkf[0:7, 1152:2048]
    g_gain_attn[...] = pkf[7:8, 0:7]
    g_gain_ffn[...] = pkf[7:8, 7:14]
    g_bias[...] = pkf[7:8, 14:23]
    for copy in sends:
        copy.wait_send()
    assert count[0] <= NSEM, count[0]


def per_device(*args):
    vmem = pl.BlockSpec(memory_space=pltpu.VMEM)
    shapes = [((T, D), BF16), ((T, D), BF16), ((1, 7), F32), ((7, D), F32), ((7, 128), F32), ((7, 128), F32),
              ((1, 9), F32), ((7, D), F32), ((1, 7), F32), ((7, FF), F32), ((7, FF), F32), ((38, D), F32)]
    results = pl.pallas_call(
        body,
        out_shape=tuple(jax.ShapeDtypeStruct(shape, dtype) for shape, dtype in shapes),
        in_specs=[vmem] * 13,
        out_specs=(vmem,) * 12,
        scratch_shapes=[pltpu.VMEM(shape, dtype) for shape, dtype in SCRATCH.values()]
        + [pltpu.SemaphoreType.DMA((NSEM,)), pltpu.SemaphoreType.DMA((NSEM,))],
        compiler_params=pltpu.CompilerParams(
            collective_id=0, has_side_effects=True, vmem_limit_bytes=60 * 2**20),
        name="layer",
    )(*(v.reshape(1, -1) if v.ndim == 1 else v for v in args))
    return tuple(v.reshape(-1) if v.shape[0] == 1 else v for v in results)


def solution(mesh):
    both = P(("dp", "ctx"))
    rows = P(("dp", "ctx"), None)
    return jax.shard_map(
        per_device,
        mesh=mesh,
        in_specs=(rows, both, both, rows, rows, rows, both, rows, both, rows, rows, rows, rows),
        out_specs=(rows, rows, both, rows, rows, rows, both, rows, both, rows, rows, rows),
        check_vma=False,
    )
```

time: 3440 us -> 163 us (0.05)
  blocking collectives: 2100 us -> 0 us
  waiting for transfers between devices: 811 us -> 0 us
  starting transfers between devices: 231 us -> 0 us
  local copies, waits for them, and re-layouts: 172 us -> 9.13 us
  Pallas kernels: 0 us -> 153 us
  matrix products: 85.7 us -> 0 us
    unnamed x4 -> x0, blocking collectives: 1460 us -> none
    all_gather x5 -> x0, waiting for transfers between devices: 803 us -> none  [the longest x1 306 us: per_device(): lax.all_gather(w_up, ('dp', 'ctx'), axis=0, tiled=True)]
    all_gather x5 -> x0, blocking collectives: 639 us -> none  [the longest x1 313 us: per_device(): lax.all_gather(w_value, ('dp', 'ctx'), axis=0, tiled=True)]
    unnamed x62 -> x0, starting transfers between devices: 231 us -> none
    unnamed x155 -> x34, local copies, waits for them, and re-layouts: 172 us -> 9.13 us
    pallas_call x0 -> x1, Pallas kernels: none -> 153 us  [per_device(): pl.pallas_call(body, out_shape=tuple((jax.ShapeDtypeStruct(shape, dtype)...]
    dot_general x27 -> x0, matrix products: 85.7 us -> none  [the longest x7 32.3 us: matmul_tn(): lax.dot_general(left_side, right_side, (((0,), (0,)), ((), ())), preferre...]
  transfers between devices with their start and end apart: 67 -> 0, of which waited for: 5 -> 0; matrix products, arithmetic and copies ran while one was open for 20% -> 0% of each run, Pallas kernels for 0% -> 0%
where the time goes in v1:
time: 163 us
  Pallas kernels  153 us (94%)
  local copies, waits for them, and re-layouts  9.13 us (6%)
    pallas_call x1, Pallas kernels, per_device(): pl.pallas_call(body, out_shape=tuple((jax.ShapeDtypeStruct(shape, dtype)...  153 us
    unnamed x34, local copies, waits for them, and re-layouts  9.13 us

profile of v1, /device:TPU:1, one launch (start us, length us, event | category | flops | bytes accessed | tf_op | source)
XLA Modules:
  0.0 162.8 jit_solution(5647789900713271802)
XLA Ops:
  0.6 152.9 %layer.1 = (bf16[128,896]{1,0:T(8,128)(2,1)}, bf16[128,896]{1,0:T(8,128)(2,1)}, f32[1,7]{1,0:T(1,128)}, f32[7,896]{1,0:T(8,128)}, f32[7,128]{1,0:T(8,128)}, /*in...) custom-call(bf16[128,896]{1,0:T(8,128)(2,1)} %tok.1, ...), custom_call_target="tpu_custom_call" | custom-call | tf_op jit(solution)/shard_map/layer/pallas_call | solution.py:689
  153.6 0.0 copy-start
  153.6 1.7 %copy.37 = bf16[128,896]{1,0:T(8,128)(2,1)} copy(bf16[128,896]{1,0:T(8,128)(2,1)} %get-tuple-element.48) | data formatting | bytes 458752
  155.3 0.0 copy-done
  155.3 0.0 copy-start.10
  155.3 0.0 copy-start.5
  155.3 0.0 copy-start.2
  155.3 0.7 copy.38
  156.0 0.0 copy-done.10
  156.0 0.5 copy.39
  156.5 0.0 copy-done.5
  156.5 0.0 copy-start.7
  156.5 0.0 copy-start.4
  156.5 0.6 copy.40
  157.1 0.1 copy-done.7
  157.2 0.0 copy-start.6
  157.2 0.6 copy.41
  157.8 0.1 copy-done.6
  157.9 0.0 copy-start.9
  157.9 0.6 copy.42
  158.5 0.0 copy-done.9
  158.5 0.5 copy.43
  159.0 0.0 copy-done.4
  159.0 0.0 copy-start.8
  159.0 0.6 copy.44
  159.6 0.1 copy-done.8
  159.6 0.5 copy.45
  160.2 0.0 copy-done.2
  160.2 0.0 copy-start.1
  160.2 0.7 copy.46
  160.8 0.3 copy-done.1
  161.1 0.0 copy-start.3
  161.1 0.7 copy.47
  161.8 0.3 copy-done.3
  162.1 0.7 copy.48
Async XLA Ops:
  153.6 1.7 %copy-start = (bf16[128,896]{1,0:T(8,128)(2,1)S(1)}, bf16[128,896]{1,0:T(8,128)(2,1)}, u32[]{:S(2)}) copy-start(bf16[128,896]{1,0:T(8,128)(2,1)} %get-tuple-element.49) | copy-start | bytes 688132
  155.3 0.7 copy-start.10
  155.3 1.2 copy-start.5
  155.3 4.9 %copy-start.2 = (f32[7,4864]{1,0:T(8,128)S(1)}, f32[7,4864]{1,0:T(8,128)}, u32[]{:S(2)}) copy-start(f32[7,4864]{1,0:T(8,128)} %get-tuple-element.57) | copy-start | bytes 408580
  156.5 0.7 copy-start.7
  156.5 2.5 %copy-start.4 = (f32[7,896]{1,0:T(8,128)S(1)}, f32[7,896]{1,0:T(8,128)}, u32[]{:S(2)}) copy-start(f32[7,896]{1,0:T(8,128)} %get-tuple-element.55) | copy-start | bytes 75268
  157.2 0.7 copy-start.6
  157.9 0.6 copy-start.9
  159.0 0.7 copy-start.8
  160.2 1.0 copy-start.1
  161.1 1.0 copy-start.3

commit v2 on v1

v2 whole, which is shorter than its diff:
```python
import functools

import jax
import jax.numpy as jnp
import numpy as np
from jax import lax
from jax.experimental import pallas as pl
from jax.experimental.pallas import tpu as pltpu
from jax.sharding import PartitionSpec as P

F32 = jnp.float32
BF16 = jnp.bfloat16
MESH = pl.DeviceIdType.MESH
D = 896
DP = 1024
FF = 4864
FS = 640
T = 128
VEC = 2 * D + 1152
EPS = 1e-6
MASKED = -1e9
LANES = (0, 128, 256, 384, 896, 1280, 1408, 1536, 512, 640, 768, 1024, 1152, 1664, 1792, 1920)
QUERY, KEY, VALUE, OUT = (0, 1, 2, 3, 8, 9, 10), 4, 11, (12, 5, 6, 7, 13, 14, 15)
GATHER1 = ((0, 2, "xzy"), (2, 1, "zxy"), (3, 1, "yxz"), (4, 1, "yzx"))
GATHER2 = ((5, 1, "xzy"), (6, 1, "zxy"), (7, 1, "yxz"))
REDUCE = (((5, 2, "xzy"), (7, 1, "zxy")), ((0, 2, "xzy"), (2, 1, "zxy")), ((3, 1, "yxz"), (4, 1, "yzx")))


def iota(shape, axis):
    return lax.broadcasted_iota(jnp.int32, shape, axis)


def sevenths(v):
    return lax.shift_right_logical(v * 9363, 16)


def ninths(v):
    return lax.shift_right_logical(v * 7282, 16)


def slot_of(i):
    return (i >> 5) * 32 + ((i >> 2) & 3) * 8 + (i & 1) * 4 + ((i >> 4) & 1) * 2 + ((i >> 1) & 1)


def one_hot(test):
    return jnp.where(test, 1.0, 0.0).astype(BF16)


def mm(a, b):
    return jnp.dot(a, b, preferred_element_type=F32)


def mm_nt(a, b):
    return lax.dot_general(a, b, (((1,), (1,)), ((), ())), preferred_element_type=F32)


def mm_tn(a, b):
    return lax.dot_general(a, b, (((0,), (0,)), ((), ())), preferred_element_type=F32)


def split(v):
    hi = v.astype(BF16)
    return hi, (v - hi.astype(F32)).astype(BF16)


INPUTS = dict(
    tok=((T, D), BF16), seg=((1, T), jnp.int32), gain_attn=((1, 7), BF16), wq=((7, D), BF16), wk=((7, 128), BF16),
    wv=((7, 128), BF16), bias_qkv=((1, 9), BF16), wo=((7, D), BF16), gain_ffn=((1, 7), BF16), wgate=((7, FF), BF16),
    wup=((7, FF), BF16), wdown=((38, D), BF16), cot=((T, D), BF16),
)
OUTPUTS = dict(
    out=((T, D), BF16), ing=((T, D), BF16), g_gain_attn=((1, 7), F32), g_wq=((7, D), F32), g_wk=((7, 128), F32),
    g_wv=((7, 128), F32), g_bias=((1, 9), F32), g_wo=((7, D), F32), g_gain_ffn=((1, 7), F32), g_gate=((7, FF), F32),
    g_up=((7, FF), F32), g_down=((38, D), F32),
)
SCRATCH = dict(
    pkf=((8, 2048), F32),
    pk=((8, 16, 128), BF16),
    pkr=((8, 16, 128), BF16),
    aw=((16, 4, 4, 4, 16, 128), BF16),
    guf=((2, 8, 8, FS), F32),
    gus=((8, 16, FS), BF16),
    gui=((8, 16, FS), BF16),
    wf=((2, 56, FS), F32),
    wg=((4, 4, 56, FS), BF16),
    wu=((4, 4, 56, FS), BF16),
    da=((4, 4, 40, 512), BF16),
    db=((4, 4, 40, 384), BF16),
    pad=((D, DP), BF16),
    perm=((D, D), BF16),
    order=((FS, FS), BF16),
    pick=((32, VEC), BF16),
    mask=((128, VEC), BF16),
    wdf=((40, D), F32),
    segs=((2, 8, 128), jnp.int32),
    kv=((2, T, 256), BF16),
    prob=((14, T, 256), F32),
    ball=((4, 2, T, D), BF16),
    yall=((4, 2, T, D), BF16),
    mb=((4, 2 * T, FS), BF16),
    dgb=((4, 2 * T, FS), BF16),
    dub=((4, 2 * T, FS), BF16),
    po=((4, 2, T, D), BF16),
    pd=((4, 2, T, D), BF16),
    qo=((4, T, D), BF16),
    qd=((4, T, D), BF16),
    ro=((3, T, D), BF16),
    rd=((3, T, D), BF16),
    gg=((4, 4, 56, FS), BF16),
    gu=((4, 4, 56, FS), BF16),
    ga=((4, 4, 40, 512), BF16),
    gb=((4, 4, 40, 384), BF16),
    rg1=((3, 4, 56, FS), BF16),
    ru1=((3, 4, 56, FS), BF16),
    ra1=((3, 4, 40, 512), BF16),
    rb1=((3, 4, 40, 384), BF16),
    sg1=((4, 56, FS), BF16),
    su1=((4, 56, FS), BF16),
    sa1=((4, 40, 512), BF16),
    sb1=((4, 40, 384), BF16),
    rg2=((3, 56, FS), BF16),
    ru2=((3, 56, FS), BF16),
    ra2=((3, 40, 512), BF16),
    rb2=((3, 40, 384), BF16),
    fs=((8, 2, 8, FS), F32),
    fr=((8, 2, 8, FS), F32),
    dkv=((2, T, 256), BF16),
    dkvf=((2, T, 256), F32),
    dkr=((T, 256), BF16),
    gat=((16, 4, 4, 4, 16, 128), BF16),
    gar=((8, 4, 4, 4, 16, 128), BF16),
    r1=((3, 8, 4, 4, 16, 128), BF16),
    t2=((8, 4, 4, 16, 128), BF16),
    r2=((3, 8, 4, 16, 128), BF16),
    t3=((8, 4, 16, 128), BF16),
    r3=((3, 8, 16, 128), BF16),
    fin=((8, 16, 128), F32),
    finr=((8, 8, 128), F32),
)
NSEM = 270


def body(*refs):
    sizes = (len(INPUTS), len(OUTPUTS), len(SCRATCH), len(INPUTS), len(OUTPUTS), 4)
    parts = []
    for size in sizes:
        parts.append(refs[sum(map(len, parts)):][:size])
    s = dict(zip(SCRATCH, parts[2]))
    i_ = dict(zip(INPUTS, parts[3]))
    o_ = dict(zip(OUTPUTS, parts[4]))
    ssem, rsem, isem, osem = parts[5]
    loads = {
        name: pltpu.make_async_copy(ref, i_[name], isem.at[n]) for n, (name, ref) in enumerate(zip(INPUTS, parts[0]))}
    stores = {
        name: pltpu.make_async_copy(o_[name], ref, osem.at[n]) for n, (name, ref) in enumerate(zip(OUTPUTS, parts[1]))}

    def load(*names):
        for name in names:
            loads[name].wait()
        return [i_[name][...] for name in names]

    def store(name, value):
        o_[name][...] = value
        stores[name].start()

    count = [0]
    sends = []
    di, yh = lax.axis_index("dp"), lax.axis_index("ctx")
    c, z, yl, x = di % 2, (di // 2) % 4, (di // 8) % 2, di // 16
    y = yh * 2 + yl
    here = {"x": x, "y": y, "z": z}

    def device(x, y, z, c):
        return (((x * 2 + y % 2) * 4 + z) * 2 + c, y // 2)

    def along(axis, k):
        at = dict(here)
        at[axis] = (at[axis] + k) % 4
        return device(at["x"], at["y"], at["z"], c)

    sibling = device(x, y, z, 1 - c)

    def remote(src, dst, dev):
        n = count[0]
        count[0] += 1
        copy = pltpu.make_async_remote_copy(
            src_ref=src, dst_ref=dst, send_sem=ssem.at[n], recv_sem=rsem.at[n],
            device_id=dev, device_id_type=MESH)
        copy.start()
        sends.append(copy)
        return copy

    def landed(copies):
        for copy in copies:
            copy.wait_recv()

    barrier = pltpu.get_barrier_semaphore()
    partners = [along(axis, k) for axis in "xyz" for k in (1, 2, 3)] + [sibling]
    partners += [device(x, (y + k) % 4, z, 1 - c) for k in (1, 2, 3)]
    for dev in partners:
        pl.semaphore_signal(barrier, inc=1, device_id=dev, device_id_type=MESH)

    for name in ("wgate", "wup", "wq", "wk", "wv", "wo", "gain_attn", "gain_ffn", "bias_qkv", "wdown", "seg", "cot", "tok"):
        loads[name].start()

    pad, perm, order, pick, mask = s["pad"], s["perm"], s["order"], s["pick"], s["mask"]
    r = iota((FS, 1), 0)
    u = lax.shift_right_logical(r * 1725, 16)
    target = (u & 3) * 160 + (u >> 2) * 40 + (r - u * 38)
    order[...] = one_hot((iota((FS, FS), 1) == target) & (r < 608))
    guf = s["guf"]
    guf[...] = jnp.zeros(guf.shape, F32)

    load("wgate", "wup")
    for k in range(8):
        guf[0, k, 0:7, 0:608] = i_["wgate"][:, 608 * k:608 * k + 608].astype(F32)
        guf[1, k, 0:7, 0:608] = i_["wup"][:, 608 * k:608 * k + 608].astype(F32)
    placed = mm(guf[...].reshape(128, FS).astype(BF16), order[...]).reshape(2, 4, 2, 8, FS)
    lane = iota((32, FS), 1)
    for q in range(4):
        piece = jnp.zeros((32, FS), F32)
        for xx in range(4):
            moved = placed[:, xx].reshape(32, FS)
            if xx != q:
                moved = pltpu.roll(moved, (160 * (xx - q)) % FS, 1)
            piece = jnp.where((lane >= 160 * xx) & (lane < 160 * xx + 160), moved, piece)
        piece = piece.reshape(2, 2, 8, FS)
        for yy in range(2):
            s["gus"][(2 * (q % 2) + yy) * 2 + q // 2] = jnp.concatenate(
                [piece[0, yy], piece[1, yy]], axis=0).astype(BF16)
    me8 = y * 2 + c
    s["gui"][me8] = s["gus"][me8]
    pkf = s["pkf"]
    wq, wk, wv, wo, gain_attn, gain_ffn, bias_qkv = load(
        "wq", "wk", "wv", "wo", "gain_attn", "gain_ffn", "bias_qkv")
    pkf[0:7, 0:896] = wq.astype(F32)
    pkf[0:7, 896:1024] = wk.astype(F32)
    pkf[0:7, 1024:1152] = wv.astype(F32)
    pkf[0:7, 1152:2048] = wo.astype(F32)
    pkf[7:8, :] = jnp.zeros((1, 2048), F32)
    pkf[7:8, 896:903] = gain_attn.astype(F32)
    pkf[7:8, 903:910] = gain_ffn.astype(F32)
    pkf[7:8, 910:919] = bias_qkv.astype(F32)
    for t in range(8):
        s["pk"][t] = jnp.concatenate(
            [pkf[:, at:at + 128] for at in (LANES[t], LANES[8 + t])], axis=0).astype(BF16)
    wdf = s["wdf"]
    (wdown,) = load("wdown")
    wdf[0:38] = wdown.astype(F32)
    wdf[38:40] = jnp.zeros((2, D), F32)
    s["da"][x, z] = wdf[:, 0:512].astype(BF16)
    s["db"][x, z] = wdf[:, 512:896].astype(BF16)
    (seg,) = load("seg")
    s["segs"][yh] = jnp.broadcast_to(seg, (8, 128))

    pl.semaphore_wait(barrier, len(partners))
    swap = remote(s["pk"], s["pkr"], sibling)

    def slab(name, axes, **index):
        return s[name].at[tuple(index.get(a, here[a]) for a in "xz")]

    def ffn_first(names):
        copies = []
        for name, axes in names:
            part = slab(name, axes)
            copies += [remote(part, part, along(axes[0], k)) for k in (1, 3, 2)]
        return copies

    def ffn_near(names):
        copies = []
        for name, axes in names:
            part = slab(name, axes, **{axes[0]: slice(None)})
            copies += [remote(part, part, along(axes[1], k)) for k in (1, 3)]
        return copies

    def ffn_far(names, near):
        copies = []
        for at, (name, axes) in enumerate(names):
            for h, k in enumerate((1, 3)):
                near[2 * at + h].wait_recv()
                part = slab(name, axes, **{axes[0]: pl.ds(2 * h, 2), axes[1]: (here[axes[1]] - k) % 4})
                copies.append(remote(part, part, along(axes[1], k)))
        return copies

    DOWN, WIDE = (("da", "xz"), ("db", "zx")), (("wg", "xz"), ("wu", "zx"))
    gu_in = []
    for k in (2, 1, 3, 0):
        for e in range(2):
            if k or e:
                ty, tc = (y + k) % 4, (c + e) % 2
                gu_in.append(remote(s["gus"].at[ty * 2 + tc], s["gui"].at[me8], device(x, ty, z, tc)))
    down1 = ffn_first(DOWN)
    seg_copy = remote(s["segs"].at[yh], s["segs"].at[yh], along("y", 2))

    swap.wait_recv()
    for t in range(8):
        own, other = s["pk"][t].astype(F32), s["pkr"][t].astype(F32)
        first = jnp.concatenate([own[0:8], other[0:8]], axis=0)
        second = jnp.concatenate([other[8:16], own[8:16]], axis=0)
        s["aw"][8 * c + t, x, z, y] = jnp.where(c == 0, first, second).astype(BF16)

    def slots(name, start, runs, axes, **index):
        at = [index.get(a, slice(None) if a in axes else here[a]) for a in "xzy"]
        return s[name].at[(pl.ds(start, runs),) + tuple(at)]

    def attn_phase(group, phase):
        copies = []
        for start, runs, axes in group:
            part = slots("aw", 8 * c + start, runs, axes[:phase])
            copies += [remote(part, part, along(axes[phase], k)) for k in (1, 2, 3)]
        return copies

    first1 = attn_phase(GATHER1, 0)
    first2 = attn_phase(GATHER2, 0)

    landed(gu_in)
    for at in range(8):
        both = s["gui"][at].astype(F32)
        s["wf"][0, 7 * at:7 * at + 7] = both[0:7]
        s["wf"][1, 7 * at:7 * at + 7] = both[8:15]
    s["wg"][x, z] = s["wf"][0].astype(BF16)
    s["wu"][x, z] = s["wf"][1].astype(BF16)
    wide1 = ffn_first(WIDE)
    landed(first1)
    second1 = attn_phase(GATHER1, 1)
    landed(first2)
    second2 = attn_phase(GATHER2, 1)
    landed(down1)
    down2 = ffn_near(DOWN)
    for at in range(0, D, 128):
        d = iota((128, 1), 0) + at
        i = sevenths(d)
        pad[at:at + 128] = one_hot(iota((128, DP), 1) == slot_of(i) * 8 + (d - i * 7))
        perm[at:at + 128] = one_hot(iota((128, D), 1) == slot_of(i) * 7 + (d - i * 7))
    landed(second1)
    third1 = attn_phase(GATHER1, 2)
    landed(wide1)
    wide2 = ffn_near(WIDE)
    landed(second2)
    third2 = attn_phase(GATHER2, 2)

    (tok,) = load("tok")
    xf = tok.astype(F32)
    (cot,) = load("cot")
    s["yall"][y, c] = cot
    r1 = lax.rsqrt(jnp.mean(xf * xf, axis=-1, keepdims=True) + EPS)
    seg_copy.wait_recv()
    rows0 = s["segs"][0][0:1].astype(F32)
    rows1 = s["segs"][1][0:1].astype(F32)
    own_row = jnp.where(yh == 0, rows0, rows1)
    diag = iota((T, T), 0) == iota((T, T), 1)
    own_seg = jnp.sum(jnp.where(diag, own_row, 0.0), axis=1, keepdims=True)
    length = jnp.sum(2.0 * T - jnp.sum(rows0 + rows1, axis=1, keepdims=True), axis=0, keepdims=True)
    base = (yh * T).astype(F32)
    place = iota((T, 128), 0).astype(F32) + base
    lane128 = iota((T, 128), 1)
    expo = (lane128 % 32).astype(F32) * (-2.0 / 64.0)
    freq = jnp.exp(expo * float(np.log(1e6)))
    angle = (place - own_seg * length) * freq
    cosine = jnp.cos(angle)
    low_half = lane128 % 64 < 32
    sine = jnp.where(low_half, -jnp.sin(angle), jnp.sin(angle))

    def swapped(v):
        return jnp.where(low_half, pltpu.roll(v, 96, 1), pltpu.roll(v, 32, 1))

    key_seg = jnp.concatenate([rows0, rows1], axis=1)
    key_at = iota((T, 256), 1)
    query_at = iota((T, 256), 0) + yh * T
    allowed = (key_seg == own_seg) & (key_at <= query_at)
    last_rows = one_hot(iota((128, DP), 1) == iota((128, DP), 0) * 8 + 7)
    n = iota((1, VEC), 1)
    d = jnp.where(n >= D, n - D, n)
    i = sevenths(d)
    m = n - 2 * D
    im = ninths(m)
    lane_of = jnp.where(m >= 0, 14 + m - im * 9, d - i * 7 + jnp.where(n >= D, 7, 0))
    pick[...] = one_hot(iota((32, VEC), 0) == lane_of)
    mask[...] = one_hot(iota((128, VEC), 0) == slot_of(jnp.where(m >= 0, im, i)))

    def pass_on(group, arrivals):
        copies = []
        for start, runs, axes in group:
            part = slots("aw", 8 * c + start, runs, axes[:2])
            copies.append(remote(part, part, sibling))
        for k in (1, 2, 3):
            for at, (start, runs, axes) in enumerate(group):
                arrivals[3 * at + k - 1].wait_recv()
                part = slots("aw", 8 * c + start, runs, axes[:2], **{axes[2]: (here[axes[2]] - k) % 4})
                copies.append(remote(part, part, sibling))
        return copies

    landed(pass_on(GATHER1, third1))

    def weight(*tiles):
        return jnp.concatenate([s["aw"][g].reshape(DP, 128) for g in tiles], axis=1)

    picked = mm(last_rows, weight(KEY))[:, 0:32].astype(BF16)
    vecs = jnp.sum(mm(picked, pick[...]) * mask[...].astype(F32), axis=0, keepdims=True)
    gain_a, gain_f, bias = vecs[:, 0:D], vecs[:, D:2 * D], vecs[:, 2 * D:]

    a = (xf * r1 * gain_a).astype(BF16)
    a_pad = mm(a, pad[...]).astype(BF16)
    qkv = mm(a_pad, weight(*QUERY, KEY, VALUE)) + bias

    def tile(t):
        return qkv[:, 128 * t:128 * t + 128]

    def rope(v):
        return v * cosine + swapped(v) * sine

    key_tile = rope(tile(7)).astype(BF16)
    value_tile = tile(8).astype(BF16)
    s["kv"][yh] = jnp.concatenate([key_tile, value_tile], axis=1)
    kv_copy = remote(s["kv"].at[yh], s["kv"].at[yh], along("y", 2))
    q_tiles = [rope(tile(t)).astype(BF16) for t in range(7)]

    ring = count[0]
    passed = ring + 8
    count[0] += 16

    def arriving(name, k):
        n = ring + k + 4 * (name == "yall")
        mine = s[name].at[y, c]
        return pltpu.make_async_remote_copy(
            src_ref=mine, dst_ref=mine, send_sem=ssem.at[n], recv_sem=rsem.at[n],
            device_id=along("y", 4 - k), device_id_type=MESH)

    def passing(name, k):
        n = passed + k + 4 * (name == "yall")
        part = s[name].at[(y + k) % 4, c]
        return pltpu.make_async_remote_copy(
            src_ref=part, dst_ref=part, send_sem=ssem.at[n], recv_sem=rsem.at[n],
            device_id=sibling, device_id_type=MESH)

    passing("yall", 0).start()
    for k in (1, 3, 2):
        arriving("yall", k).start()
    forward2 = pass_on(GATHER2, third2)
    down3 = ffn_far(DOWN, down2)
    wide3 = ffn_far(WIDE, wide2)
    kv_copy.wait_recv()
    kv = s["kv"][...].reshape(256, 256).astype(F32)
    lane256 = iota((256, 128), 1)

    def halves(v):
        turned = pltpu.roll(v, 64, 1)
        lo, hi = lane256 < 64, lane256 >= 64
        pick2 = lambda m, u: jnp.where(m, u, 0.0).astype(BF16)
        return ((pick2(lo, v), pick2(hi, turned)), (pick2(lo, turned), pick2(hi, v)))

    keys = halves(kv[:, 0:128])
    values = halves(kv[:, 128:256])
    mixed = []
    for t in range(7):
        total = None
        for e in range(2):
            h = 2 * t + e
            logits = jnp.where(allowed, mm_nt(q_tiles[t], keys[h // 7][e]) * 0.125, MASKED)
            top = jnp.max(logits, axis=-1, keepdims=True)
            raw = jnp.exp(logits - top)
            pr = raw / jnp.sum(raw, axis=-1, keepdims=True)
            s["prob"][h] = pr
            part = mm(pr.astype(BF16), values[h // 7][e])
            total = part if total is None else total + part
        mixed.append(total.astype(BF16))
    mixed = jnp.concatenate(mixed, axis=1)
    o_pad = mm(mixed, pad[...]).astype(BF16)
    landed(forward2)
    hidden = xf + mm(o_pad, weight(*OUT))
    r2 = lax.rsqrt(jnp.mean(hidden * hidden, axis=-1, keepdims=True) + EPS)
    b = (hidden * r2 * gain_f).astype(BF16)
    s["ball"][y, c] = mm(b, perm[...]).astype(BF16)
    passing("ball", 0).start()
    for k in (1, 3, 2):
        arriving("ball", k).start()
    landed(down3 + wide3)
    base = count[0]
    count[0] += 16

    def chunk_copies(k):
        yy = (y + k) % 4
        copies = []
        for j, (part, got, ring) in enumerate((("pd", "qd", "rd"), ("po", "qo", "ro"))):
            n = base + 8 * j + k
            copies.append(pltpu.make_async_remote_copy(
                src_ref=s[part].at[yy, 1 - c], dst_ref=s[got].at[yy], send_sem=ssem.at[n], recv_sem=rsem.at[n],
                device_id=sibling, device_id_type=MESH))
            copies.append(pltpu.make_async_remote_copy(
                src_ref=s[part].at[yy, c], dst_ref=s[ring].at[k - 1], send_sem=ssem.at[n + 4],
                recv_sem=rsem.at[n + 4], device_id=along("y", k), device_id_type=MESH))
        return copies

    def turn(step):
        return step + (step // 2) * (5 - 2 * step)

    def chunk(step, carry):
        k = turn(step)
        passing("ball", k).wait_recv()
        passing("yall", k).wait_recv()
        d_sib, d_ring, o_sib, o_ring = chunk_copies(k)
        yy = (y + k) % 4
        bt = s["ball"][yy].reshape(2 * T, D)
        yt = s["yall"][yy].reshape(2 * T, D)
        gate_w, up_w = s["wg"][...].reshape(D, FS), s["wu"][...].reshape(D, FS)
        down_a, down_b = s["da"][...].reshape(FS, 512), s["db"][...].reshape(FS, 384)
        gate, up = mm(bt, gate_w), mm(bt, up_w)
        sg = 1.0 / (1.0 + jnp.exp(-gate))
        silu = gate * sg
        m = (silu * up).astype(BF16)
        dm = mm_nt(yt[:, 0:512], down_a) + mm_nt(yt[:, 512:896], down_b)
        dgate = (dm * up * sg * (1.0 + gate * (1.0 - sg))).astype(BF16)
        dup = (dm * silu).astype(BF16)
        s["mb"][yy], s["dgb"][yy], s["dub"][yy] = m, dgate, dup
        s["pd"][yy] = (mm_nt(dgate, gate_w) + mm_nt(dup, up_w)).astype(BF16).reshape(2, T, D)
        d_sib.start()
        s["po"][yy, :, :, 0:512] = mm(m, down_a).astype(BF16).reshape(2, T, 512)
        s["po"][yy, :, :, 512:896] = mm(m, down_b).astype(BF16).reshape(2, T, 384)
        o_sib.start()

        @pl.when(step < 3)
        def _():
            for name in ("yall", "ball"):
                arriving(name, turn(step + 1)).wait_recv()
                passing(name, turn(step + 1)).start()

        d_sib.wait_recv()
        s["pd"][yy, c] = (s["pd"][yy, c].astype(F32) + s["qd"][yy].astype(F32)).astype(BF16)

        @pl.when(step > 0)
        def _():
            d_ring.start()

        return carry

    lax.fori_loop(0, 4, chunk, 0)
    for name in ("ball", "yall"):
        sends.extend([passing(name, k) for k in range(4)] + [arriving(name, k) for k in (1, 2, 3)])
    red_d, red_o = [], []
    for k in range(4):
        d_sib, d_ring, o_sib, o_ring = chunk_copies(k)
        sends.extend([d_sib, o_sib])
        o_sib.wait_recv()
        yy = (y + k) % 4
        s["po"][yy, c] = (s["po"][yy, c].astype(F32) + s["qo"][yy].astype(F32)).astype(BF16)
        if k:
            o_ring.start()
            sends.extend([d_ring, o_ring])
            red_d.append(d_ring)
            red_o.append(o_ring)

    ball = s["ball"][...].reshape(1024, D)
    s["gg"][...] = mm_tn(ball, s["dgb"][...].reshape(1024, FS)).astype(BF16).reshape(4, 4, 56, FS)
    s["gu"][...] = mm_tn(ball, s["dub"][...].reshape(1024, FS)).astype(BF16).reshape(4, 4, 56, FS)
    down = mm_tn(s["mb"][...].reshape(1024, FS), s["yall"][...].reshape(1024, D))
    s["ga"][...] = down[:, 0:512].reshape(4, 4, 40, 512).astype(BF16)
    s["gb"][...] = down[:, 512:896].reshape(4, 4, 40, 384).astype(BF16)
    FG = (("gg", "rg1", "sg1", "rg2", "zx"), ("gu", "ru1", "su1", "ru2", "xz"),
          ("ga", "ra1", "sa1", "ra2", "zx"), ("gb", "rb1", "sb1", "rb2", "xz"))

    def plane(ref, axis, index):
        return ref.at[index] if axis == "x" else ref.at[:, index]


    def piece(name, axes, **index):
        return tuple(index.get(a, slice(None)) for a in "xz")

    half = []
    for src, r_1, s_1, r_2, axes in FG:
        for h, k in enumerate((1, 3)):
            part = s[src].at[piece(src, axes, **{axes[0]: (here[axes[0]] + 2) % 4, axes[1]: pl.ds(2 * h, 2)})]
            half.append(remote(part, s[r_1].at[2, pl.ds(2 * h, 2)], along(axes[0], k)))

    landed(red_d)
    db_pad = s["pd"][y, c].astype(F32)
    for k in (1, 2, 3):
        db_pad = db_pad + s["rd"][k - 1].astype(F32)
    hi, lo = split(db_pad)
    dbv = mm_nt(hi, perm[...]) + mm_nt(lo, perm[...])
    gain_f_grad = jnp.sum(dbv * hidden * r2, axis=0, keepdims=True)
    ev = dbv * gain_f
    inner = jnp.mean(ev * hidden, axis=-1, keepdims=True)
    dh = cot.astype(F32) + r2 * ev - hidden * (r2 * r2 * r2 * inner)
    dh_low = dh.astype(BF16)

    def grad(tiles, value):
        for at, g in enumerate(tiles):
            s["gat"][g] = value[:, 128 * at:128 * at + 128].astype(BF16).reshape(4, 4, 4, 16, 128)

    def reduce_start(group):
        start, runs = group[0][0], sum(run[1] for run in group)
        return remote(
            s["gat"].at[pl.ds(8 * (1 - c) + start, runs)], s["gar"].at[pl.ds(start, runs)], sibling)

    def cut(axes, axis, index):
        kept = [a for a in "xzy" if a in axes]
        return tuple(index if a == axis else slice(None) for a in kept)

    def reduce_send(group, src, dst, phase):
        copies = []
        for start, runs, axes in group:
            left, axis = axes[:3 - phase], axes[2 - phase]
            first = 8 * c + start if src == "gat" else start
            for k in (1, 2, 3):
                part = s[src].at[(pl.ds(first, runs),) + cut(left, axis, (here[axis] + k) % 4)]
                copies.append(remote(part, s[dst].at[k - 1, pl.ds(start, runs)], along(axis, k)))
        return copies

    def reduce_sum(group, src, dst, phase, copies):
        landed(copies)
        for start, runs, axes in group:
            left, axis = axes[:3 - phase], axes[2 - phase]
            for t in range(start, start + runs):
                first = 8 * c + t if src == "gat" else t
                total = s[src][(first,) + cut(left, axis, here[axis])].astype(F32)
                for k in range(3):
                    total = total + s[dst][k, t].astype(F32)
                yield t, total

    def reduce_0(group, copy):
        copy.wait_recv()
        start, runs = group[0][0], sum(run[1] for run in group)
        for t in range(start, start + runs):
            s["gat"][8 * c + t] = (s["gat"][8 * c + t].astype(F32) + s["gar"][t].astype(F32)).astype(BF16)
        return reduce_send(group, "gat", "r1", 0)

    def reduce_1(group, copies):
        for t, total in reduce_sum(group, "gat", "r1", 0, copies):
            s["t2"][t] = total.astype(BF16)
        return reduce_send(group, "t2", "r2", 1)

    def reduce_2(group, copies):
        for t, total in reduce_sum(group, "t2", "r2", 1, copies):
            s["t3"][t] = total.astype(BF16)
        return reduce_send(group, "t3", "r3", 2)

    def reduce_3(group, copies):
        for t, total in reduce_sum(group, "t3", "r3", 2, copies):
            s["fin"][t] = total

    grad(OUT, mm_tn(o_pad, dh_low))
    part_o = reduce_start(REDUCE[0])
    do_pad = mm_nt(dh_low, weight(*OUT))
    do = mm_nt(do_pad.astype(BF16), pad[...]).astype(BF16)

    dk = [[None, None], [None, None]]
    dv = [[None, None], [None, None]]
    dq_tiles = []
    for t in range(7):
        if t == 1:
            part_o = reduce_0(REDUCE[0], part_o)
        if t == 2:
            fg1 = []
            for at, (src, r_1, s_1, r_2, axes) in enumerate(FG):
                for h, k in enumerate((1, 3)):
                    half[2 * at + h].wait_recv()
                    there = (here[axes[0]] + k) % 4
                    part = piece(src, axes, **{axes[0]: there, axes[1]: pl.ds(2 * h, 2)})
                    s[src][part] = (s[src][part].astype(F32) + s[r_1][2, 2 * h:2 * h + 2].astype(F32)).astype(BF16)
                    part = s[src].at[piece(src, axes, **{axes[0]: there})]
                    fg1.append(remote(part, s[r_1].at[h], along(axes[0], k)))
        do_t = do[:, 128 * t:128 * t + 128]
        total = None
        for e in range(2):
            h = 2 * t + e
            g = h // 7
            pr = s["prob"][h]
            dpr = mm_nt(do_t, values[g][e])
            ds = (pr * (dpr - jnp.sum(pr * dpr, axis=-1, keepdims=True)) * 0.125).astype(BF16)
            part = mm(ds, keys[g][e])
            total = part if total is None else total + part
            kp, vp = mm_tn(ds, q_tiles[t]), mm_tn(pr.astype(BF16), do_t)
            dk[g][e] = kp if dk[g][e] is None else dk[g][e] + kp
            dv[g][e] = vp if dv[g][e] is None else dv[g][e] + vp
        dq_tiles.append((total * cosine - swapped(total) * sine).astype(BF16))

    def gather(parts):
        lo = parts[0][0] + pltpu.roll(parts[0][1], 64, 1)
        hi = parts[1][1] + pltpu.roll(parts[1][0], 64, 1)
        return jnp.where(lane256 < 64, lo, hi)

    dkv = jnp.concatenate([gather(dk), gather(dv)], axis=1).reshape(2, T, 256)
    s["dkvf"][...] = dkv
    s["dkv"][...] = dkv.astype(BF16)
    dkv_copy = remote(s["dkv"].at[1 - yh], s["dkr"], along("y", 2))

    dq = jnp.concatenate(dq_tiles, axis=1)
    grad(QUERY, mm_tn(a_pad, dq))
    part_q = reduce_start(REDUCE[1])
    da_pad = mm_nt(dq, weight(*QUERY))
    part_q = reduce_0(REDUCE[1], part_q)
    dkv_copy.wait_recv()
    dkv_own = s["dkvf"][yh] + s["dkr"][...].astype(F32)
    dko, dvl = dkv_own[:, 0:128], dkv_own[:, 128:256].astype(BF16)
    dkl = (dko * cosine - swapped(dko) * sine).astype(BF16)
    dkvl = jnp.concatenate([dkl, dvl], axis=1)
    da_pad = da_pad + mm_nt(dkvl, weight(KEY, VALUE))
    hi, lo = split(da_pad)
    dav = mm_nt(hi, pad[...]) + mm_nt(lo, pad[...])
    gain_a_grad = jnp.sum(dav * xf * r1, axis=0, keepdims=True)
    bias_grad = jnp.sum(jnp.concatenate([dq, dkvl], axis=1).astype(F32), axis=0, keepdims=True)
    small = jnp.concatenate([gain_a_grad, gain_f_grad, bias_grad], axis=1)
    spread = (mask[...].astype(F32) * small).astype(BF16)
    small_rows = mm_nt(spread, pick[...]).astype(BF16)
    small_rows = mm_tn(last_rows, jnp.concatenate([small_rows, jnp.zeros((128, 96), BF16)], axis=1))
    kv_grad = mm_tn(a_pad, dkvl)
    grad((KEY,), kv_grad[:, 0:128] + small_rows)
    grad((VALUE,), kv_grad[:, 128:256])
    part_k = reduce_start(REDUCE[2])

    fv = dav * gain_a
    inner = jnp.mean(fv * xf, axis=-1, keepdims=True)
    store("ing", (dh + r1 * fv - xf * (r1 * r1 * r1 * inner)).astype(BF16))

    landed(fg1)
    fg2 = []
    for src, r_1, s_1, r_2, axes in FG:
        own = s[src][here["x"]] if axes[0] == "x" else s[src][:, here["z"]]
        total = own.astype(F32)
        for h in range(2):
            total = total + s[r_1][h].astype(F32)
        s[s_1][...] = total.astype(BF16)
        for k in (1, 2, 3):
            there = (here[axes[1]] + k) % 4
            fg2.append(remote(s[s_1].at[there], s[r_2].at[k - 1], along(axes[1], k)))

    part_k = reduce_0(REDUCE[2], part_k)
    part_o = reduce_1(REDUCE[0], part_o)
    landed(red_o)
    total = hidden + s["po"][y, c].astype(F32)
    for k in (1, 2, 3):
        total = total + s["ro"][k - 1].astype(F32)
    store("out", total.astype(BF16))
    part_q = reduce_1(REDUCE[1], part_q)

    landed(fg2)
    sums = []
    for src, r_1, s_1, r_2, axes in FG:
        total = s[s_1][here[axes[1]]].astype(F32)
        for k in (1, 2, 3):
            total = total + s[r_2][k - 1].astype(F32)
        sums.append(total)
    store("g_down", jnp.concatenate([sums[2][0:38], sums[3][0:38]], axis=1))
    s["wf"][0] = sums[0]
    s["wf"][1] = sums[1]
    for at in range(8):
        for g in range(2):
            s["fs"][at, g, 0:7] = s["wf"][g, 7 * at:7 * at + 7]
            s["fs"][at, g, 7:8] = jnp.zeros((1, FS), F32)
    fin_in = []
    for k in range(4):
        for e in range(2):
            if k or e:
                ty, tc = (y + k) % 4, (c + e) % 2
                fin_in.append(remote(s["fs"].at[ty * 2 + tc], s["fr"].at[me8], device(x, ty, z, tc)))
    s["fr"][me8] = s["fs"][me8]

    part_o = reduce_2(REDUCE[0], part_o)
    part_k = reduce_1(REDUCE[2], part_k)
    part_q = reduce_2(REDUCE[1], part_q)

    landed(fin_in)
    for yy in range(2):
        for xx in range(4):
            block = jnp.zeros((16, FS), F32)
            lane16 = iota((16, FS), 1)
            for q in range(4):
                moved = s["fr"][(2 * (q % 2) + yy) * 2 + q // 2].reshape(16, FS)
                if xx != q:
                    moved = pltpu.roll(moved, (160 * (q - xx)) % FS, 1)
                block = jnp.where((lane16 >= 160 * q) & (lane16 < 160 * q + 160), moved, block)
            guf[:, 2 * xx + yy] = block.reshape(2, 8, FS)
    hi, lo = split(guf[...].reshape(128, FS))
    flat = (mm_nt(hi, order[...]) + mm_nt(lo, order[...])).reshape(2, 8, 8, FS)
    for g, name in enumerate(("g_gate", "g_up")):
        for k in range(8):
            o_[name][:, 608 * k:608 * k + 608] = flat[g, k, 0:7, 0:608]
        stores[name].start()

    part_k = reduce_2(REDUCE[2], part_k)
    reduce_3(REDUCE[0], part_o)
    reduce_3(REDUCE[1], part_q)
    reduce_3(REDUCE[2], part_k)
    fin_copy = remote(s["fin"].at[:, pl.ds((1 - c) * 8, 8)], s["finr"], sibling)
    fin_copy.wait_recv()
    for t in range(8):
        own = jnp.where(c == 0, s["fin"][t, 0:8], s["fin"][t, 8:16])
        other = s["finr"][t]
        pkf[:, LANES[t]:LANES[t] + 128] = jnp.where(c == 0, own, other)
        pkf[:, LANES[8 + t]:LANES[8 + t] + 128] = jnp.where(c == 0, other, own)
    store("g_wq", pkf[0:7, 0:896])
    store("g_wk", pkf[0:7, 896:1024])
    store("g_wv", pkf[0:7, 1024:1152])
    store("g_wo", pkf[0:7, 1152:2048])
    store("g_gain_attn", pkf[7:8, 896:903])
    store("g_gain_ffn", pkf[7:8, 903:910])
    store("g_bias", pkf[7:8, 910:919])
    for copy in sends:
        copy.wait_send()
    for copy in stores.values():
        copy.wait()
    assert count[0] <= NSEM, count[0]


def hand_over(*refs):
    n = len(OUTPUTS)
    copies = [pltpu.make_async_copy(refs[k], refs[n + k], refs[2 * n].at[k]) for k in range(n)]
    for copy in copies:
        copy.start()
    for copy in copies:
        copy.wait()


def per_device(*args):
    shapes = tuple(jax.ShapeDtypeStruct(*v) for v in OUTPUTS.values())
    anywhere = pl.BlockSpec(memory_space=pl.ANY)
    results = pl.pallas_call(
        body,
        out_shape=shapes,
        in_specs=[anywhere] * len(INPUTS),
        out_specs=(anywhere,) * len(OUTPUTS),
        scratch_shapes=[
            pltpu.VMEM(shape, dtype) for part in (SCRATCH, INPUTS, OUTPUTS) for shape, dtype in part.values()]
        + [pltpu.SemaphoreType.DMA((n,)) for n in (NSEM, NSEM, len(INPUTS), len(OUTPUTS))],
        compiler_params=pltpu.CompilerParams(
            collective_id=0, has_side_effects=True, vmem_limit_bytes=60 * 2**20),
        name="layer",
    )(*(v.reshape(1, -1) if v.ndim == 1 else v for v in args))
    results = pl.pallas_call(
        hand_over,
        out_shape=shapes,
        in_specs=[anywhere] * len(OUTPUTS),
        out_specs=(pl.BlockSpec(memory_space=pltpu.VMEM),) * len(OUTPUTS),
        scratch_shapes=[pltpu.SemaphoreType.DMA((len(OUTPUTS),))],
        name="results",
    )(*results)
    return tuple(v.reshape(-1) if v.shape[0] == 1 else v for v in results)


def solution(mesh):
    both = P(("dp", "ctx"))
    rows = P(("dp", "ctx"), None)
    return jax.shard_map(
        per_device,
        mesh=mesh,
        in_specs=(rows, both, both, rows, rows, rows, both, rows, both, rows, rows, rows, rows),
        out_specs=(rows, rows, both, rows, rows, rows, both, rows, both, rows, rows, rows),
        check_vma=False,
    )
```

time: 163 us -> 128 us (0.79)
  Pallas kernels: 153 us -> 127 us
  local copies, waits for them, and re-layouts: 9.13 us -> 0 us
    pallas_call x1 -> x2, Pallas kernels: 153 us -> 127 us  [the longest x1 124 us: per_device(): pl.pallas_call(body, out_shape=shapes, in_specs=[anywhere] * len(INPUTS),...]
    unnamed x34 -> x0, local copies, waits for them, and re-layouts: 9.13 us -> none
where the time goes in v2:
time: 128 us
  Pallas kernels  127 us (99%)
    pallas_call x1, Pallas kernels, per_device(): pl.pallas_call(body, out_shape=shapes, in_specs=[anywhere] * len(INPUTS),...  124 us

profile of v2, /device:TPU:1, one launch (start us, length us, event | category | flops | bytes accessed | tf_op | source)
XLA Modules:
  0.0 127.6 jit_solution(11420312833253252859)
XLA Ops:
  0.6 124.4 %layer.1 = (bf16[128,896]{1,0:T(8,128)(2,1)}, bf16[128,896]{1,0:T(8,128)(2,1)}, f32[1,7]{1,0:T(1,128)}, f32[7,896]{1,0:T(8,128)}, f32[7,128]{1,0:T(8,128)}, /*in...) custom-call(bf16[128,896]{1,0:T(8,128)(2,1)} %refs_0_.1, ...), custom_call_target="tpu_custom_call" | custom-call | tf_op jit(solution)/shard_map/layer/pallas_call | solution.py:817
  125.1 2.4 %results.1 = (bf16[128,896]{1,0:T(8,128)(2,1)}, bf16[128,896]{1,0:T(8,128)(2,1)}, f32[1,7]{1,0:T(1,128)}, f32[7,896]{1,0:T(8,128)}, f32[7,128]{1,0:T(8,128)}, /*...) custom-call(bf16[128,896]{1,0:T(8,128)(2,1)} %get-tuple-element.36.r, ...), custom_call_target="tpu_custom_call" | custom-call | tf_op jit(solution)/shard_map/results/pallas_call | solution.py:829

commit v3 on v2

--- a/solution.py
+++ b/solution.py
@@ -19,11 +19,11 @@
 VEC = 2 * D + 1152
 EPS = 1e-6
 MASKED = -1e9
-LANES = (0, 128, 256, 384, 896, 1280, 1408, 1536, 512, 640, 768, 1024, 1152, 1664, 1792, 1920)
-QUERY, KEY, VALUE, OUT = (0, 1, 2, 3, 8, 9, 10), 4, 11, (12, 5, 6, 7, 13, 14, 15)
+LANES = (0, 128, 256, 384, 896, 1280, 1408, 1536, 512, 640, 768, 1152, 1024, 1664, 1792, 1920)
+QUERY, KEY, VALUE, OUT = (0, 1, 2, 3, 8, 9, 10), 4, 12, (11, 5, 6, 7, 13, 14, 15)
 GATHER1 = ((0, 2, "xzy"), (2, 1, "zxy"), (3, 1, "yxz"), (4, 1, "yzx"))
 GATHER2 = ((5, 1, "xzy"), (6, 1, "zxy"), (7, 1, "yxz"))
-REDUCE = (((5, 2, "xzy"), (7, 1, "zxy")), ((0, 2, "xzy"), (2, 1, "zxy")), ((3, 1, "yxz"), (4, 1, "yzx")))
+REDUCE = (((5, 1, "xzy"), (6, 1, "yxz"), (7, 1, "yzx")), ((0, 2, "xzy"), (2, 1, "yxz"), (3, 1, "yzx")), ((4, 1, "yxz"),))
 
 
 def iota(shape, axis):
@@ -122,8 +122,8 @@
     ru2=((3, 56, FS), BF16),
     ra2=((3, 40, 512), BF16),
     rb2=((3, 40, 384), BF16),
-    fs=((8, 2, 8, FS), F32),
-    fr=((8, 2, 8, FS), F32),
+    fs=((8, 16, FS), BF16),
+    fr=((8, 16, FS), BF16),
     dkv=((2, T, 256), BF16),
     dkvf=((2, T, 256), F32),
     dkr=((T, 256), BF16),
@@ -137,7 +137,7 @@
     fin=((8, 16, 128), F32),
     finr=((8, 8, 128), F32),
 )
-NSEM = 270
+NSEM = 100
 
 
 def body(*refs):
@@ -164,7 +164,6 @@
         stores[name].start()
 
     count = [0]
-    sends = []
     di, yh = lax.axis_index("dp"), lax.axis_index("ctx")
     c, z, yl, x = di % 2, (di // 2) % 4, (di // 8) % 2, di // 16
     y = yh * 2 + yl
@@ -180,19 +179,38 @@
 
     sibling = device(x, y, z, 1 - c)
 
-    def remote(src, dst, dev):
-        n = count[0]
-        count[0] += 1
+    def fresh(n=1):
+        count[0] += n
+        return count[0] - n
+
+    VIEWS = dict(
+        tile=s["aw"].reshape(1024, 16, 128), wide=s["wg"], da=s["da"], db=s["db"], seg=s["segs"], piece=s["gui"], kv=s["kv"], rows=s["ball"].reshape(8, T, D),
+        fin=s["finr"])
+    groups = []
+
+    def group(kind):
+        groups.append([kind, fresh(), 0])
+        return groups[-1]
+
+    def remote(src, dst, dev, to, slots):
         copy = pltpu.make_async_remote_copy(
-            src_ref=src, dst_ref=dst, send_sem=ssem.at[n], recv_sem=rsem.at[n],
+            src_ref=src, dst_ref=dst, send_sem=ssem.at[to[1]], recv_sem=rsem.at[to[1]],
             device_id=dev, device_id_type=MESH)
         copy.start()
-        sends.append(copy)
-        return copy
-
-    def landed(copies):
-        for copy in copies:
-            copy.wait_recv()
+        to[2] += slots
+
+    def wait_for(sems, to):
+        whole, n = VIEWS[to[0]], to[2]
+        if to[0] in ("wide", "da", "db"):
+            fours = {2: (1, 2), 3: (1, 3), 4: (1, 4), 6: (2, 3), 8: (2, 4)}[n]
+            whole = whole.at[pl.ds(0, fours[0]), pl.ds(0, fours[1])]
+        else:
+            whole = whole.at[pl.ds(0, n)]
+        pltpu.make_async_copy(whole, whole, sems.at[to[1]]).wait()
+
+    def landed(*arrivals):
+        for to in arrivals:
+            wait_for(rsem, to)
 
     barrier = pltpu.get_barrier_semaphore()
     partners = [along(axis, k) for axis in "xyz" for k in (1, 2, 3)] + [sibling]
@@ -250,49 +268,73 @@
     wdf[38:40] = jnp.zeros((2, D), F32)
     s["da"][x, z] = wdf[:, 0:512].astype(BF16)
     s["db"][x, z] = wdf[:, 512:896].astype(BF16)
+    (cot,) = load("cot")
+    s["yall"][y, c] = cot
     (seg,) = load("seg")
     s["segs"][yh] = jnp.broadcast_to(seg, (8, 128))
 
     pl.semaphore_wait(barrier, len(partners))
-    swap = remote(s["pk"], s["pkr"], sibling)
+    swap = group("tile")
+    remote(s["pk"], s["pkr"], sibling, swap, 8)
 
     def slab(name, axes, **index):
         return s[name].at[tuple(index.get(a, here[a]) for a in "xz")]
 
-    def ffn_first(names):
-        copies = []
-        for name, axes in names:
-            part = slab(name, axes)
-            copies += [remote(part, part, along(axes[0], k)) for k in (1, 3, 2)]
-        return copies
-
-    def ffn_near(names):
-        copies = []
-        for name, axes in names:
-            part = slab(name, axes, **{axes[0]: slice(None)})
-            copies += [remote(part, part, along(axes[1], k)) for k in (1, 3)]
-        return copies
-
-    def ffn_far(names, near):
-        copies = []
-        for at, (name, axes) in enumerate(names):
-            for h, k in enumerate((1, 3)):
-                near[2 * at + h].wait_recv()
-                part = slab(name, axes, **{axes[0]: pl.ds(2 * h, 2), axes[1]: (here[axes[1]] - k) % 4})
-                copies.append(remote(part, part, along(axes[1], k)))
-        return copies
-
-    DOWN, WIDE = (("da", "xz"), ("db", "zx")), (("wg", "xz"), ("wu", "zx"))
-    gu_in = []
+    KIND = dict(wg="wide", wu="wide", da="da", db="db")
+
+    def ffn_first(name, axes, to):
+        part = slab(name, axes)
+        for k in (1, 3, 2):
+            remote(part, part, along(axes[0], k), to, 1)
+
+    def ffn_near(name, axes):
+        near = [group(KIND[name]), group(KIND[name])]
+        part = slab(name, axes, **{axes[0]: slice(None)})
+        for h, k in enumerate((1, 3)):
+            remote(part, part, along(axes[1], k), near[h], 4)
+        return near
+
+    def ffn_far(name, axes, near):
+        to = group(KIND[name])
+        for h, k in enumerate((1, 3)):
+            landed(near[h])
+            part = slab(name, axes, **{axes[0]: pl.ds(2 * h, 2), axes[1]: (here[axes[1]] - k) % 4})
+            remote(part, part, along(axes[1], k), to, 2)
+        return to
+
+    gu_in = group("piece")
     for k in (2, 1, 3, 0):
         for e in range(2):
             if k or e:
                 ty, tc = (y + k) % 4, (c + e) % 2
-                gu_in.append(remote(s["gus"].at[ty * 2 + tc], s["gui"].at[me8], device(x, ty, z, tc)))
-    down1 = ffn_first(DOWN)
-    seg_copy = remote(s["segs"].at[yh], s["segs"].at[yh], along("y", 2))
-
-    swap.wait_recv()
+                remote(s["gus"].at[ty * 2 + tc], s["gui"].at[me8], device(x, ty, z, tc), gu_in, 1)
+    first_a, first_b, wide1 = group("da"), group("db"), group("wide")
+    ffn_first("da", "xz", first_a)
+    ffn_first("db", "zx", first_b)
+    seg_copy = group("seg")
+    remote(s["segs"].at[yh], s["segs"].at[yh], along("y", 2), seg_copy, 1)
+    ring = fresh(16)
+    passed = ring + 8
+
+    def arriving(name, k):
+        n = ring + k + 4 * (name == "yall")
+        mine = s[name].at[y, c]
+        return pltpu.make_async_remote_copy(
+            src_ref=mine, dst_ref=mine, send_sem=ssem.at[n], recv_sem=rsem.at[n],
+            device_id=along("y", 4 - k), device_id_type=MESH)
+
+    def passing(name, k):
+        n = passed + k + 4 * (name == "yall")
+        part = s[name].at[(y + k) % 4, c]
+        return pltpu.make_async_remote_copy(
+            src_ref=part, dst_ref=part, send_sem=ssem.at[n], recv_sem=rsem.at[n],
+            device_id=sibling, device_id_type=MESH)
+
+    passing("yall", 0).start()
+    for k in (1, 3):
+        arriving("yall", k).start()
+
+    landed(swap)
     for t in range(8):
         own, other = s["pk"][t].astype(F32), s["pkr"][t].astype(F32)
         first = jnp.concatenate([own[0:8], other[0:8]], axis=0)
@@ -303,16 +345,26 @@
         at = [index.get(a, slice(None) if a in axes else here[a]) for a in "xzy"]
         return s[name].at[(pl.ds(start, runs),) + tuple(at)]
 
-    def attn_phase(group, phase):
-        copies = []
-        for start, runs, axes in group:
+    def attn_phase(tiles, phase):
+        arrivals = [group("tile") for _ in range(3 if phase == 2 else 1)]
+        for start, runs, axes in tiles:
             part = slots("aw", 8 * c + start, runs, axes[:phase])
-            copies += [remote(part, part, along(axes[phase], k)) for k in (1, 2, 3)]
-        return copies
+            for k in (1, 2, 3):
+                remote(part, part, along(axes[phase], k), arrivals[(k - 1) % len(arrivals)], runs * 4 ** phase)
+        return arrivals
 
     first1 = attn_phase(GATHER1, 0)
     first2 = attn_phase(GATHER2, 0)
-
+    for at in range(0, D, 128):
+        d = iota((128, 1), 0) + at
+        i = sevenths(d)
+        pad[at:at + 128] = one_hot(iota((128, DP), 1) == slot_of(i) * 8 + (d - i * 7))
+        perm[at:at + 128] = one_hot(iota((128, D), 1) == slot_of(i) * 7 + (d - i * 7))
+
+    landed(*first1)
+    second1 = attn_phase(GATHER1, 1)
+    landed(*first2)
+    second2 = attn_phase(GATHER2, 1)
     landed(gu_in)
     for at in range(8):
         both = s["gui"][at].astype(F32)
@@ -320,31 +372,21 @@
         s["wf"][1, 7 * at:7 * at + 7] = both[8:15]
     s["wg"][x, z] = s["wf"][0].astype(BF16)
     s["wu"][x, z] = s["wf"][1].astype(BF16)
-    wide1 = ffn_first(WIDE)
-    landed(first1)
-    second1 = attn_phase(GATHER1, 1)
-    landed(first2)
-    second2 = attn_phase(GATHER2, 1)
-    landed(down1)
-    down2 = ffn_near(DOWN)
-    for at in range(0, D, 128):
-        d = iota((128, 1), 0) + at
-        i = sevenths(d)
-        pad[at:at + 128] = one_hot(iota((128, DP), 1) == slot_of(i) * 8 + (d - i * 7))
-        perm[at:at + 128] = one_hot(iota((128, D), 1) == slot_of(i) * 7 + (d - i * 7))
-    landed(second1)
+    ffn_first("wg", "xz", wide1)
+    ffn_first("wu", "zx", wide1)
+    landed(*second1)
     third1 = attn_phase(GATHER1, 2)
+    landed(first_a, first_b)
+    near_a, near_b = ffn_near("da", "xz"), ffn_near("db", "zx")
+    landed(*second2)
+    third2 = attn_phase(GATHER2, 2)
     landed(wide1)
-    wide2 = ffn_near(WIDE)
-    landed(second2)
-    third2 = attn_phase(GATHER2, 2)
+    near_g, near_u = ffn_near("wg", "xz"), ffn_near("wu", "zx")
 
     (tok,) = load("tok")
     xf = tok.astype(F32)
-    (cot,) = load("cot")
-    s["yall"][y, c] = cot
     r1 = lax.rsqrt(jnp.mean(xf * xf, axis=-1, keepdims=True) + EPS)
-    seg_copy.wait_recv()
+    landed(seg_copy)
     rows0 = s["segs"][0][0:1].astype(F32)
     rows1 = s["segs"][1][0:1].astype(F32)
     own_row = jnp.where(yh == 0, rows0, rows1)
@@ -378,19 +420,29 @@
     pick[...] = one_hot(iota((32, VEC), 0) == lane_of)
     mask[...] = one_hot(iota((128, VEC), 0) == slot_of(jnp.where(m >= 0, im, i)))
 
-    def pass_on(group, arrivals):
-        copies = []
-        for start, runs, axes in group:
+    def pass_on(tiles, arrivals, between=None):
+        to = group("tile")
+        for start, runs, axes in tiles:
             part = slots("aw", 8 * c + start, runs, axes[:2])
-            copies.append(remote(part, part, sibling))
-        for k in (1, 2, 3):
-            for at, (start, runs, axes) in enumerate(group):
-                arrivals[3 * at + k - 1].wait_recv()
+            remote(part, part, sibling, to, 16 * runs)
+        for k in (1, 3, 2):
+            if k == 2 and between:
+                between()
+            landed(arrivals[k - 1])
+            for start, runs, axes in tiles:
                 part = slots("aw", 8 * c + start, runs, axes[:2], **{axes[2]: (here[axes[2]] - k) % 4})
-                copies.append(remote(part, part, sibling))
-        return copies
-
-    landed(pass_on(GATHER1, third1))
+                remote(part, part, sibling, to, 16 * runs)
+        return to
+
+    far = []
+
+    def down_far():
+        far.append(ffn_far("da", "xz", near_a))
+        far.append(ffn_far("db", "zx", near_b))
+
+    forward1 = pass_on(GATHER1, third1, down_far)
+    far.append(ffn_far("wg", "xz", near_g))
+    landed(forward1)
 
     def weight(*tiles):
         return jnp.concatenate([s["aw"][g].reshape(DP, 128) for g in tiles], axis=1)
@@ -406,40 +458,21 @@
     def tile(t):
         return qkv[:, 128 * t:128 * t + 128]
 
+
     def rope(v):
         return v * cosine + swapped(v) * sine
 
     key_tile = rope(tile(7)).astype(BF16)
     value_tile = tile(8).astype(BF16)
     s["kv"][yh] = jnp.concatenate([key_tile, value_tile], axis=1)
-    kv_copy = remote(s["kv"].at[yh], s["kv"].at[yh], along("y", 2))
+    kv_copy = group("kv")
+    remote(s["kv"].at[yh], s["kv"].at[yh], along("y", 2), kv_copy, 1)
     q_tiles = [rope(tile(t)).astype(BF16) for t in range(7)]
 
-    ring = count[0]
-    passed = ring + 8
-    count[0] += 16
-
-    def arriving(name, k):
-        n = ring + k + 4 * (name == "yall")
-        mine = s[name].at[y, c]
-        return pltpu.make_async_remote_copy(
-            src_ref=mine, dst_ref=mine, send_sem=ssem.at[n], recv_sem=rsem.at[n],
-            device_id=along("y", 4 - k), device_id_type=MESH)
-
-    def passing(name, k):
-        n = passed + k + 4 * (name == "yall")
-        part = s[name].at[(y + k) % 4, c]
-        return pltpu.make_async_remote_copy(
-            src_ref=part, dst_ref=part, send_sem=ssem.at[n], recv_sem=rsem.at[n],
-            device_id=sibling, device_id_type=MESH)
-
-    passing("yall", 0).start()
-    for k in (1, 3, 2):
-        arriving("yall", k).start()
+    arriving("yall", 2).start()
+    far.append(ffn_far("wu", "zx", near_u))
     forward2 = pass_on(GATHER2, third2)
-    down3 = ffn_far(DOWN, down2)
-    wide3 = ffn_far(WIDE, wide2)
-    kv_copy.wait_recv()
+    landed(kv_copy)
     kv = s["kv"][...].reshape(256, 256).astype(F32)
     lane256 = iota((256, 128), 1)
 
@@ -472,23 +505,24 @@
     b = (hidden * r2 * gain_f).astype(BF16)
     s["ball"][y, c] = mm(b, perm[...]).astype(BF16)
     passing("ball", 0).start()
-    for k in (1, 3, 2):
+    for k in (1, 3):
         arriving("ball", k).start()
-    landed(down3 + wide3)
-    base = count[0]
-    count[0] += 16
+    landed(*far)
+    base = fresh(4)
+    red_d, sib_o = group("rows"), group("rows")
+    red_o = [group("rows") for _ in range(4)]
 
     def chunk_copies(k):
         yy = (y + k) % 4
         copies = []
-        for j, (part, got, ring) in enumerate((("pd", "qd", "rd"), ("po", "qo", "ro"))):
-            n = base + 8 * j + k
+        for part, got, ring_in, sib, out_sem in (
+                ("pd", "qd", "rd", base + k, red_d[1]), ("po", "qo", "ro", sib_o[1], red_o[0][1] + k)):
             copies.append(pltpu.make_async_remote_copy(
-                src_ref=s[part].at[yy, 1 - c], dst_ref=s[got].at[yy], send_sem=ssem.at[n], recv_sem=rsem.at[n],
+                src_ref=s[part].at[yy, 1 - c], dst_ref=s[got].at[yy], send_sem=ssem.at[sib], recv_sem=rsem.at[sib],
                 device_id=sibling, device_id_type=MESH))
             copies.append(pltpu.make_async_remote_copy(
-                src_ref=s[part].at[yy, c], dst_ref=s[ring].at[k - 1], send_sem=ssem.at[n + 4],
-                recv_sem=rsem.at[n + 4], device_id=along("y", k), device_id_type=MESH))
+                src_ref=s[part].at[yy, c], dst_ref=s[ring_in].at[(k + 2) % 3], send_sem=ssem.at[out_sem],
+                recv_sem=rsem.at[out_sem], device_id=along("y", k), device_id_type=MESH))
         return copies
 
     def turn(step):
@@ -518,60 +552,101 @@
         s["po"][yy, :, :, 512:896] = mm(m, down_b).astype(BF16).reshape(2, T, 384)
         o_sib.start()
 
+        @pl.when(step == 0)
+        def _():
+            arriving("ball", 2).start()
+
         @pl.when(step < 3)
         def _():
             for name in ("yall", "ball"):
                 arriving(name, turn(step + 1)).wait_recv()
                 passing(name, turn(step + 1)).start()
 
+        @pl.when(step > 0)
+        def _():
+            finish(turn(step - 1))
+
+        return carry
+
+    def finish(k):
+        d_sib, d_ring, _, _ = chunk_copies(k)
+        yy = (y + k) % 4
         d_sib.wait_recv()
         s["pd"][yy, c] = (s["pd"][yy, c].astype(F32) + s["qd"][yy].astype(F32)).astype(BF16)
 
-        @pl.when(step > 0)
+        @pl.when(k > 0)
         def _():
             d_ring.start()
 
-        return carry
-
     lax.fori_loop(0, 4, chunk, 0)
-    for name in ("ball", "yall"):
-        sends.extend([passing(name, k) for k in range(4)] + [arriving(name, k) for k in (1, 2, 3)])
-    red_d, red_o = [], []
-    for k in range(4):
-        d_sib, d_ring, o_sib, o_ring = chunk_copies(k)
-        sends.extend([d_sib, o_sib])
-        o_sib.wait_recv()
-        yy = (y + k) % 4
-        s["po"][yy, c] = (s["po"][yy, c].astype(F32) + s["qo"][yy].astype(F32)).astype(BF16)
-        if k:
-            o_ring.start()
-            sends.extend([d_ring, o_ring])
-            red_d.append(d_ring)
-            red_o.append(o_ring)
-
-    ball = s["ball"][...].reshape(1024, D)
-    s["gg"][...] = mm_tn(ball, s["dgb"][...].reshape(1024, FS)).astype(BF16).reshape(4, 4, 56, FS)
-    s["gu"][...] = mm_tn(ball, s["dub"][...].reshape(1024, FS)).astype(BF16).reshape(4, 4, 56, FS)
+    finish(turn(3))
+    red_d[2], sib_o[2] = 3, 4
+
+    FG = {"ga": ("ra1", "sa1", "ra2", "zx", "da"), "gb": ("rb1", "sb1", "rb2", "xz", "db"),
+          "gg": ("rg1", "sg1", "rg2", "zx", "wide"), "gu": ("ru1", "su1", "ru2", "xz", "wide")}
+
+    def piece(**index):
+        return tuple(index.get(a, slice(None)) for a in "xz")
+
+    def fold(src):
+        r_1, _, _, axes, kind = FG[src]
+        half = [group(kind), group(kind)]
+        for h, k in enumerate((1, 3)):
+            part = s[src].at[piece(**{axes[0]: (here[axes[0]] + 2) % 4, axes[1]: pl.ds(2 * h, 2)})]
+            remote(part, s[r_1].at[2, pl.ds(2 * h, 2)], along(axes[0], k), half[h], 2)
+        return half
+
+    def spread_out(src, half):
+        r_1, _, _, axes, kind = FG[src]
+        to = group(kind)
+        for h, k in enumerate((1, 3)):
+            landed(half[h])
+            there = (here[axes[0]] + k) % 4
+            part = piece(**{axes[0]: there, axes[1]: pl.ds(2 * h, 2)})
+            s[src][part] = (s[src][part].astype(F32) + s[r_1][2, 2 * h:2 * h + 2].astype(F32)).astype(BF16)
+            remote(s[src].at[piece(**{axes[0]: there})], s[r_1].at[h], along(axes[0], k), to, 4)
+        return to
+
+    def second_axis(src, arrived):
+        r_1, s_1, r_2, axes, kind = FG[src]
+        landed(arrived)
+        total = s[src][piece(**{axes[0]: here[axes[0]]})].astype(F32)
+        for h in range(2):
+            total = total + s[r_1][h].astype(F32)
+        s[s_1][...] = total.astype(BF16)
+        to = group(kind)
+        for k in (1, 2, 3):
+            remote(s[s_1].at[(here[axes[1]] + k) % 4], s[r_2].at[k - 1], along(axes[1], k), to, 1)
+        return to
+
+    def owned(src, arrived):
+        _, s_1, r_2, axes, _ = FG[src]
+        landed(arrived)
+        total = s[s_1][here[axes[1]]].astype(F32)
+        for k in range(3):
+            total = total + s[r_2][k].astype(F32)
+        return total
+
     down = mm_tn(s["mb"][...].reshape(1024, FS), s["yall"][...].reshape(1024, D))
     s["ga"][...] = down[:, 0:512].reshape(4, 4, 40, 512).astype(BF16)
     s["gb"][...] = down[:, 512:896].reshape(4, 4, 40, 384).astype(BF16)
-    FG = (("gg", "rg1", "sg1", "rg2", "zx"), ("gu", "ru1", "su1", "ru2", "xz"),
-          ("ga", "ra1", "sa1", "ra2", "zx"), ("gb", "rb1", "sb1", "rb2", "xz"))
-
-    def plane(ref, axis, index):
-        return ref.at[index] if axis == "x" else ref.at[:, index]
-
-
-    def piece(name, axes, **index):
-        return tuple(index.get(a, slice(None)) for a in "xz")
-
-    half = []
-    for src, r_1, s_1, r_2, axes in FG:
-        for h, k in enumerate((1, 3)):
-            part = s[src].at[piece(src, axes, **{axes[0]: (here[axes[0]] + 2) % 4, axes[1]: pl.ds(2 * h, 2)})]
-            half.append(remote(part, s[r_1].at[2, pl.ds(2 * h, 2)], along(axes[0], k)))
+    fg = {src: fold(src) for src in ("ga", "gb")}
+    ball = s["ball"][...].reshape(1024, D)
+    s["gg"][...] = mm_tn(ball, s["dgb"][...].reshape(1024, FS)).astype(BF16).reshape(4, 4, 56, FS)
+    fg["gg"] = fold("gg")
+    s["gu"][...] = mm_tn(ball, s["dub"][...].reshape(1024, FS)).astype(BF16).reshape(4, 4, 56, FS)
+    fg["gu"] = fold("gu")
+    for src in ("ga", "gb"):
+        fg[src] = spread_out(src, fg[src])
+    landed(sib_o)
+    for k in range(4):
+        yy = (y + k) % 4
+        s["po"][yy, c] = (s["po"][yy, c].astype(F32) + s["qo"][yy].astype(F32)).astype(BF16)
 
     landed(red_d)
+    for k in (1, 3):
+        chunk_copies(k)[3].start()
+        red_o[k][2] = 1
     db_pad = s["pd"][y, c].astype(F32)
     for k in (1, 2, 3):
         db_pad = db_pad + s["rd"][k - 1].astype(F32)
@@ -587,28 +662,29 @@
         for at, g in enumerate(tiles):
             s["gat"][g] = value[:, 128 * at:128 * at + 128].astype(BF16).reshape(4, 4, 4, 16, 128)
 
-    def reduce_start(group):
-        start, runs = group[0][0], sum(run[1] for run in group)
-        return remote(
-            s["gat"].at[pl.ds(8 * (1 - c) + start, runs)], s["gar"].at[pl.ds(start, runs)], sibling)
+    def reduce_start(tiles):
+        start, runs = tiles[0][0], sum(run[1] for run in tiles)
+        to = group("tile")
+        remote(s["gat"].at[pl.ds(8 * (1 - c) + start, runs)], s["gar"].at[pl.ds(start, runs)], sibling, to, 64 * runs)
+        return to
 
     def cut(axes, axis, index):
         kept = [a for a in "xzy" if a in axes]
         return tuple(index if a == axis else slice(None) for a in kept)
 
-    def reduce_send(group, src, dst, phase):
-        copies = []
-        for start, runs, axes in group:
+    def reduce_send(tiles, src, dst, phase):
+        to = group("tile")
+        for start, runs, axes in tiles:
             left, axis = axes[:3 - phase], axes[2 - phase]
             first = 8 * c + start if src == "gat" else start
             for k in (1, 2, 3):
                 part = s[src].at[(pl.ds(first, runs),) + cut(left, axis, (here[axis] + k) % 4)]
-                copies.append(remote(part, s[dst].at[k - 1, pl.ds(start, runs)], along(axis, k)))
-        return copies
-
-    def reduce_sum(group, src, dst, phase, copies):
-        landed(copies)
-        for start, runs, axes in group:
+                remote(part, s[dst].at[k - 1, pl.ds(start, runs)], along(axis, k), to, runs * 4 ** (2 - phase))
+        return to
+
+    def reduce_sum(tiles, src, dst, phase, arrived):
+        landed(arrived)
+        for start, runs, axes in tiles:
             left, axis = axes[:3 - phase], axes[2 - phase]
             for t in range(start, start + runs):
                 first = 8 * c + t if src == "gat" else t
@@ -617,62 +693,55 @@
                     total = total + s[dst][k, t].astype(F32)
                 yield t, total
 
-    def reduce_0(group, copy):
-        copy.wait_recv()
-        start, runs = group[0][0], sum(run[1] for run in group)
+    def reduce_0(tiles, arrived):
+        landed(arrived)
+        start, runs = tiles[0][0], sum(run[1] for run in tiles)
         for t in range(start, start + runs):
             s["gat"][8 * c + t] = (s["gat"][8 * c + t].astype(F32) + s["gar"][t].astype(F32)).astype(BF16)
-        return reduce_send(group, "gat", "r1", 0)
-
-    def reduce_1(group, copies):
-        for t, total in reduce_sum(group, "gat", "r1", 0, copies):
+        return reduce_send(tiles, "gat", "r1", 0)
+
+    def reduce_1(tiles, arrived):
+        for t, total in reduce_sum(tiles, "gat", "r1", 0, arrived):
             s["t2"][t] = total.astype(BF16)
-        return reduce_send(group, "t2", "r2", 1)
-
-    def reduce_2(group, copies):
-        for t, total in reduce_sum(group, "t2", "r2", 1, copies):
+        return reduce_send(tiles, "t2", "r2", 1)
+
+    def reduce_2(tiles, arrived):
+        for t, total in reduce_sum(tiles, "t2", "r2", 1, arrived):
             s["t3"][t] = total.astype(BF16)
-        return reduce_send(group, "t3", "r3", 2)
-
-    def reduce_3(group, copies):
-        for t, total in reduce_sum(group, "t3", "r3", 2, copies):
+        return reduce_send(tiles, "t3", "r3", 2)
+
+    def reduce_3(tiles, arrived):
+        for t, total in reduce_sum(tiles, "t3", "r3", 2, arrived):
             s["fin"][t] = total
 
+    fg["gg"] = spread_out("gg", fg["gg"])
     grad(OUT, mm_tn(o_pad, dh_low))
     part_o = reduce_start(REDUCE[0])
+    fg["gu"] = spread_out("gu", fg["gu"])
     do_pad = mm_nt(dh_low, weight(*OUT))
     do = mm_nt(do_pad.astype(BF16), pad[...]).astype(BF16)
 
     dk = [[None, None], [None, None]]
     dv = [[None, None], [None, None]]
     dq_tiles = []
+    dsts = []
     for t in range(7):
         if t == 1:
             part_o = reduce_0(REDUCE[0], part_o)
-        if t == 2:
-            fg1 = []
-            for at, (src, r_1, s_1, r_2, axes) in enumerate(FG):
-                for h, k in enumerate((1, 3)):
-                    half[2 * at + h].wait_recv()
-                    there = (here[axes[0]] + k) % 4
-                    part = piece(src, axes, **{axes[0]: there, axes[1]: pl.ds(2 * h, 2)})
-                    s[src][part] = (s[src][part].astype(F32) + s[r_1][2, 2 * h:2 * h + 2].astype(F32)).astype(BF16)
-                    part = s[src].at[piece(src, axes, **{axes[0]: there})]
-                    fg1.append(remote(part, s[r_1].at[h], along(axes[0], k)))
+        if t == 4:
+            for src in ("ga", "gb"):
+                fg[src] = second_axis(src, fg[src])
         do_t = do[:, 128 * t:128 * t + 128]
-        total = None
         for e in range(2):
             h = 2 * t + e
             g = h // 7
             pr = s["prob"][h]
             dpr = mm_nt(do_t, values[g][e])
             ds = (pr * (dpr - jnp.sum(pr * dpr, axis=-1, keepdims=True)) * 0.125).astype(BF16)
-            part = mm(ds, keys[g][e])
-            total = part if total is None else total + part
+            dsts.append(ds)
             kp, vp = mm_tn(ds, q_tiles[t]), mm_tn(pr.astype(BF16), do_t)
             dk[g][e] = kp if dk[g][e] is None else dk[g][e] + kp
             dv[g][e] = vp if dv[g][e] is None else dv[g][e] + vp
-        dq_tiles.append((total * cosine - swapped(total) * sine).astype(BF16))
 
     def gather(parts):
         lo = parts[0][0] + pltpu.roll(parts[0][1], 64, 1)
@@ -682,14 +751,20 @@
     dkv = jnp.concatenate([gather(dk), gather(dv)], axis=1).reshape(2, T, 256)
     s["dkvf"][...] = dkv
     s["dkv"][...] = dkv.astype(BF16)
-    dkv_copy = remote(s["dkv"].at[1 - yh], s["dkr"], along("y", 2))
-
+    dkv_copy = group("kv")
+    remote(s["dkv"].at[1 - yh], s["dkr"], along("y", 2), dkv_copy, 1)
+
+    for t in range(7):
+        total = mm(dsts[2 * t], keys[2 * t // 7][0]) + mm(dsts[2 * t + 1], keys[(2 * t + 1) // 7][1])
+        dq_tiles.append((total * cosine - swapped(total) * sine).astype(BF16))
     dq = jnp.concatenate(dq_tiles, axis=1)
     grad(QUERY, mm_tn(a_pad, dq))
     part_q = reduce_start(REDUCE[1])
+    fg["gg"] = second_axis("gg", fg["gg"])
     da_pad = mm_nt(dq, weight(*QUERY))
     part_q = reduce_0(REDUCE[1], part_q)
-    dkv_copy.wait_recv()
+    part_o = reduce_1(REDUCE[0], part_o)
+    landed(dkv_copy)
     dkv_own = s["dkvf"][yh] + s["dkr"][...].astype(F32)
     dko, dvl = dkv_own[:, 0:128], dkv_own[:, 128:256].astype(BF16)
     dkl = (dko * cosine - swapped(dko) * sine).astype(BF16)
@@ -712,60 +787,42 @@
     inner = jnp.mean(fv * xf, axis=-1, keepdims=True)
     store("ing", (dh + r1 * fv - xf * (r1 * r1 * r1 * inner)).astype(BF16))
 
-    landed(fg1)
-    fg2 = []
-    for src, r_1, s_1, r_2, axes in FG:
-        own = s[src][here["x"]] if axes[0] == "x" else s[src][:, here["z"]]
-        total = own.astype(F32)
-        for h in range(2):
-            total = total + s[r_1][h].astype(F32)
-        s[s_1][...] = total.astype(BF16)
-        for k in (1, 2, 3):
-            there = (here[axes[1]] + k) % 4
-            fg2.append(remote(s[s_1].at[there], s[r_2].at[k - 1], along(axes[1], k)))
-
     part_k = reduce_0(REDUCE[2], part_k)
-    part_o = reduce_1(REDUCE[0], part_o)
-    landed(red_o)
-    total = hidden + s["po"][y, c].astype(F32)
-    for k in (1, 2, 3):
-        total = total + s["ro"][k - 1].astype(F32)
-    store("out", total.astype(BF16))
+    fg["gu"] = second_axis("gu", fg["gu"])
     part_q = reduce_1(REDUCE[1], part_q)
-
-    landed(fg2)
-    sums = []
-    for src, r_1, s_1, r_2, axes in FG:
-        total = s[s_1][here[axes[1]]].astype(F32)
-        for k in (1, 2, 3):
-            total = total + s[r_2][k - 1].astype(F32)
-        sums.append(total)
-    store("g_down", jnp.concatenate([sums[2][0:38], sums[3][0:38]], axis=1))
-    s["wf"][0] = sums[0]
-    s["wf"][1] = sums[1]
+    part_o = reduce_2(REDUCE[0], part_o)
+    part_k = reduce_1(REDUCE[2], part_k)
+    chunk_copies(2)[3].start()
+    red_o[2][2] = 1
+    s["wf"][0] = owned("gg", fg["gg"])
+    s["wf"][1] = owned("gu", fg["gu"])
     for at in range(8):
+        rows = []
         for g in range(2):
-            s["fs"][at, g, 0:7] = s["wf"][g, 7 * at:7 * at + 7]
-            s["fs"][at, g, 7:8] = jnp.zeros((1, FS), F32)
-    fin_in = []
+            rows += [s["wf"][g, 7 * at:7 * at + 7], jnp.zeros((1, FS), F32)]
+        s["fs"][at] = jnp.concatenate(rows, axis=0).astype(BF16)
+    fin_in = group("piece")
     for k in range(4):
         for e in range(2):
             if k or e:
                 ty, tc = (y + k) % 4, (c + e) % 2
-                fin_in.append(remote(s["fs"].at[ty * 2 + tc], s["fr"].at[me8], device(x, ty, z, tc)))
+                remote(s["fs"].at[ty * 2 + tc], s["fr"].at[me8], device(x, ty, z, tc), fin_in, 1)
     s["fr"][me8] = s["fs"][me8]
-
-    part_o = reduce_2(REDUCE[0], part_o)
-    part_k = reduce_1(REDUCE[2], part_k)
+    part_k = reduce_2(REDUCE[2], part_k)
     part_q = reduce_2(REDUCE[1], part_q)
-
+    store("g_down", jnp.concatenate([owned("ga", fg["ga"])[0:38], owned("gb", fg["gb"])[0:38]], axis=1))
+    landed(*red_o[1:])
+    total = hidden + s["po"][y, c].astype(F32)
+    for k in range(3):
+        total = total + s["ro"][k].astype(F32)
+    store("out", total.astype(BF16))
     landed(fin_in)
     for yy in range(2):
         for xx in range(4):
             block = jnp.zeros((16, FS), F32)
             lane16 = iota((16, FS), 1)
             for q in range(4):
-                moved = s["fr"][(2 * (q % 2) + yy) * 2 + q // 2].reshape(16, FS)
+                moved = s["fr"][(2 * (q % 2) + yy) * 2 + q // 2].astype(F32)
                 if xx != q:
                     moved = pltpu.roll(moved, (160 * (q - xx)) % FS, 1)
                 block = jnp.where((lane16 >= 160 * q) & (lane16 < 160 * q + 160), moved, block)
@@ -777,12 +834,12 @@
             o_[name][:, 608 * k:608 * k + 608] = flat[g, k, 0:7, 0:608]
         stores[name].start()
 
-    part_k = reduce_2(REDUCE[2], part_k)
     reduce_3(REDUCE[0], part_o)
     reduce_3(REDUCE[1], part_q)
     reduce_3(REDUCE[2], part_k)
-    fin_copy = remote(s["fin"].at[:, pl.ds((1 - c) * 8, 8)], s["finr"], sibling)
-    fin_copy.wait_recv()
+    fin_copy = group("fin")
+    remote(s["fin"].at[:, pl.ds((1 - c) * 8, 8)], s["finr"], sibling, fin_copy, 8)
+    landed(fin_copy)
     for t in range(8):
         own = jnp.where(c == 0, s["fin"][t, 0:8], s["fin"][t, 8:16])
         other = s["finr"][t]
@@ -795,8 +852,15 @@
     store("g_gain_attn", pkf[7:8, 896:903])
     store("g_gain_ffn", pkf[7:8, 903:910])
     store("g_bias", pkf[7:8, 910:919])
-    for copy in sends:
-        copy.wait_send()
+    for k in range(4):
+        chunk_copies(k)[0].wait_send()
+        for name in ("ball", "yall"):
+            passing(name, k).wait_send()
+            if k:
+                arriving(name, k).wait_send()
+    for to in groups:
+        if to[2]:
+            wait_for(ssem, to)
     for copy in stores.values():
         copy.wait()
     assert count[0] <= NSEM, count[0]

time: 128 us -> 123 us (0.961)
  Pallas kernels: 127 us -> 122 us
    pallas_call x1, Pallas kernels: 124 us -> 120 us  [per_device(): pl.pallas_call(body, out_shape=shapes, in_specs=[anywhere] * len(INPUTS),...]
where the time goes in v3:
time: 123 us
  Pallas kernels  122 us (99%)
    pallas_call x1, Pallas kernels, per_device(): pl.pallas_call(body, out_shape=shapes, in_specs=[anywhere] * len(INPUTS),...  120 us

profile of v3, /device:TPU:1, one launch (start us, length us, event | category | flops | bytes accessed | tf_op | source)
XLA Modules:
  0.0 122.8 jit_solution(10448765863532427903)
XLA Ops:
  0.6 119.6 %layer.1 = (bf16[128,896]{1,0:T(8,128)(2,1)}, bf16[128,896]{1,0:T(8,128)(2,1)}, f32[1,7]{1,0:T(1,128)}, f32[7,896]{1,0:T(8,128)}, f32[7,128]{1,0:T(8,128)}, /*in...) custom-call(bf16[128,896]{1,0:T(8,128)(2,1)} %refs_0_.1, ...), custom_call_target="tpu_custom_call" | custom-call | tf_op jit(solution)/shard_map/layer/pallas_call | solution.py:881
  120.3 2.4 %results.1 = (bf16[128,896]{1,0:T(8,128)(2,1)}, bf16[128,896]{1,0:T(8,128)(2,1)}, f32[1,7]{1,0:T(1,128)}, f32[7,896]{1,0:T(8,128)}, f32[7,128]{1,0:T(8,128)}, /*...) custom-call(bf16[128,896]{1,0:T(8,128)(2,1)} %get-tuple-element.36.r, ...), custom_call_target="tpu_custom_call" | custom-call | tf_op jit(solution)/shard_map/results/pallas_call | solution.py:893

commit v4 on v3

--- a/solution.py
+++ b/solution.py
@@ -21,9 +21,9 @@
 MASKED = -1e9
 LANES = (0, 128, 256, 384, 896, 1280, 1408, 1536, 512, 640, 768, 1152, 1024, 1664, 1792, 1920)
 QUERY, KEY, VALUE, OUT = (0, 1, 2, 3, 8, 9, 10), 4, 12, (11, 5, 6, 7, 13, 14, 15)
-GATHER1 = ((0, 2, "xzy"), (2, 1, "zxy"), (3, 1, "yxz"), (4, 1, "yzx"))
-GATHER2 = ((5, 1, "xzy"), (6, 1, "zxy"), (7, 1, "yxz"))
-REDUCE = (((5, 1, "xzy"), (6, 1, "yxz"), (7, 1, "yzx")), ((0, 2, "xzy"), (2, 1, "yxz"), (3, 1, "yzx")), ((4, 1, "yxz"),))
+GATHER1 = (((0, 3, "xzy"),), ((3, 1, "yxz"), (4, 1, "yzx")))
+GATHER2 = (((5, 2, "xzy"),), ((7, 1, "yxz"),))
+REDUCE = (((5, 1, "xzy"), (6, 1, "yxz"), (7, 1, "yzx")), ((0, 2, "xzy"), (2, 1, "yxz"), (3, 1, "yzx")), ((4, 1, "xzy"),))
 
 
 def iota(shape, axis):
@@ -134,6 +134,7 @@
     r2=((3, 8, 4, 16, 128), BF16),
     t3=((8, 4, 16, 128), BF16),
     r3=((3, 8, 16, 128), BF16),
+    rp=((15, 16, 128), BF16),
     fin=((8, 16, 128), F32),
     finr=((8, 8, 128), F32),
 )
@@ -215,6 +216,8 @@
     barrier = pltpu.get_barrier_semaphore()
     partners = [along(axis, k) for axis in "xyz" for k in (1, 2, 3)] + [sibling]
     partners += [device(x, (y + k) % 4, z, 1 - c) for k in (1, 2, 3)]
+    plane = [(i, j) for i in range(4) for j in range(4) if i or j]
+    partners += [device((x + i) % 4, y, (z + j) % 4, c) for i, j in plane if i and j]
     for dev in partners:
         pl.semaphore_signal(barrier, inc=1, device_id=dev, device_id_type=MESH)
 
@@ -353,8 +356,18 @@
                 remote(part, part, along(axes[phase], k), arrivals[(k - 1) % len(arrivals)], runs * 4 ** phase)
         return arrivals
 
-    first1 = attn_phase(GATHER1, 0)
-    first2 = attn_phase(GATHER2, 0)
+    def attn_plane(tiles):
+        to = group("tile")
+        for start, runs, axes in tiles:
+            part = slots("aw", 8 * c + start, runs, "")
+            for i, j in plane:
+                remote(part, part, device((x + i) % 4, y, (z + j) % 4, c), to, runs)
+        return to
+
+    plane1 = attn_plane(GATHER1[0])
+    first1 = attn_phase(GATHER1[1], 0)
+    plane2 = attn_plane(GATHER2[0])
+    first2 = attn_phase(GATHER2[1], 0)
     for at in range(0, D, 128):
         d = iota((128, 1), 0) + at
         i = sevenths(d)
@@ -362,9 +375,11 @@
         perm[at:at + 128] = one_hot(iota((128, D), 1) == slot_of(i) * 7 + (d - i * 7))
 
     landed(*first1)
-    second1 = attn_phase(GATHER1, 1)
+    second1 = attn_phase(GATHER1[1], 1)
+    landed(plane1)
+    third1y = attn_phase(GATHER1[0], 2)
     landed(*first2)
-    second2 = attn_phase(GATHER2, 1)
+    second2 = attn_phase(GATHER2[1], 1)
     landed(gu_in)
     for at in range(8):
         both = s["gui"][at].astype(F32)
@@ -375,11 +390,13 @@
     ffn_first("wg", "xz", wide1)
     ffn_first("wu", "zx", wide1)
     landed(*second1)
-    third1 = attn_phase(GATHER1, 2)
+    third1 = attn_phase(GATHER1[1], 2)
     landed(first_a, first_b)
     near_a, near_b = ffn_near("da", "xz"), ffn_near("db", "zx")
     landed(*second2)
-    third2 = attn_phase(GATHER2, 2)
+    third2 = attn_phase(GATHER2[1], 2)
+    landed(plane2)
+    third2y = attn_phase(GATHER2[0], 2)
     landed(wide1)
     near_g, near_u = ffn_near("wg", "xz"), ffn_near("wu", "zx")
 
@@ -440,9 +457,9 @@
         far.append(ffn_far("da", "xz", near_a))
         far.append(ffn_far("db", "zx", near_b))
 
-    forward1 = pass_on(GATHER1, third1, down_far)
+    forward1 = [pass_on(GATHER1[1], third1), pass_on(GATHER1[0], third1y, down_far)]
     far.append(ffn_far("wg", "xz", near_g))
-    landed(forward1)
+    landed(*forward1)
 
     def weight(*tiles):
         return jnp.concatenate([s["aw"][g].reshape(DP, 128) for g in tiles], axis=1)
@@ -471,7 +488,7 @@
 
     arriving("yall", 2).start()
     far.append(ffn_far("wu", "zx", near_u))
-    forward2 = pass_on(GATHER2, third2)
+    forward2 = [pass_on(GATHER2[1], third2), pass_on(GATHER2[0], third2y)]
     landed(kv_copy)
     kv = s["kv"][...].reshape(256, 256).astype(F32)
     lane256 = iota((256, 128), 1)
@@ -499,7 +516,7 @@
         mixed.append(total.astype(BF16))
     mixed = jnp.concatenate(mixed, axis=1)
     o_pad = mm(mixed, pad[...]).astype(BF16)
-    landed(forward2)
+    landed(*forward2)
     hidden = xf + mm(o_pad, weight(*OUT))
     r2 = lax.rsqrt(jnp.mean(hidden * hidden, axis=-1, keepdims=True) + EPS)
     b = (hidden * r2 * gain_f).astype(BF16)
@@ -791,7 +808,11 @@
     fg["gu"] = second_axis("gu", fg["gu"])
     part_q = reduce_1(REDUCE[1], part_q)
     part_o = reduce_2(REDUCE[0], part_o)
-    part_k = reduce_1(REDUCE[2], part_k)
+    for t, total in reduce_sum(REDUCE[2], "gat", "r1", 0, part_k):
+        s["t2"][t] = total.astype(BF16)
+    part_k = group("tile")
+    for n, (i, j) in enumerate(plane):
+        remote(s["t2"].at[4, (x + i) % 4, (z + j) % 4], s["rp"].at[n], device((x + i) % 4, y, (z + j) % 4, c), part_k, 1)
     chunk_copies(2)[3].start()
     red_o[2][2] = 1
     s["wf"][0] = owned("gg", fg["gg"])
@@ -808,7 +829,6 @@
                 ty, tc = (y + k) % 4, (c + e) % 2
                 remote(s["fs"].at[ty * 2 + tc], s["fr"].at[me8], device(x, ty, z, tc), fin_in, 1)
     s["fr"][me8] = s["fs"][me8]
-    part_k = reduce_2(REDUCE[2], part_k)
     part_q = reduce_2(REDUCE[1], part_q)
     store("g_down", jnp.concatenate([owned("ga", fg["ga"])[0:38], owned("gb", fg["gb"])[0:38]], axis=1))
     landed(*red_o[1:])
@@ -836,7 +856,11 @@
 
     reduce_3(REDUCE[0], part_o)
     reduce_3(REDUCE[1], part_q)
-    reduce_3(REDUCE[2], part_k)
+    landed(part_k)
+    total = s["t2"][4, x, z].astype(F32)
+    for n in range(15):
+        total = total + s["rp"][n].astype(F32)
+    s["fin"][4] = total
     fin_copy = group("fin")
     remote(s["fin"].at[:, pl.ds((1 - c) * 8, 8)], s["finr"], sibling, fin_copy, 8)
     landed(fin_copy)

time: 123 us -> 122 us (level)
  no operation moved by 1% of the time
where the time goes in v4:
time: 122 us
  Pallas kernels  121 us (99%)
    pallas_call x1, Pallas kernels, per_device(): pl.pallas_call(body, out_shape=shapes, in_specs=[anywhere] * len(INPUTS),...  119 us

profile of v4, /device:TPU:1, one launch (start us, length us, event | category | flops | bytes accessed | tf_op | source)
XLA Modules:
  0.0 122.0 jit_solution(14363185661368313161)
XLA Ops:
  0.6 118.8 %layer.1 = (bf16[128,896]{1,0:T(8,128)(2,1)}, bf16[128,896]{1,0:T(8,128)(2,1)}, f32[1,7]{1,0:T(1,128)}, f32[7,896]{1,0:T(8,128)}, f32[7,128]{1,0:T(8,128)}, /*in...) custom-call(bf16[128,896]{1,0:T(8,128)(2,1)} %refs_0_.1, ...), custom_call_target="tpu_custom_call" | custom-call | tf_op jit(solution)/shard_map/layer/pallas_call | solution.py:905
  119.4 2.4 %results.1 = (bf16[128,896]{1,0:T(8,128)(2,1)}, bf16[128,896]{1,0:T(8,128)(2,1)}, f32[1,7]{1,0:T(1,128)}, f32[7,896]{1,0:T(8,128)}, f32[7,128]{1,0:T(8,128)}, /*...) custom-call(bf16[128,896]{1,0:T(8,128)(2,1)} %get-tuple-element.36.r, ...), custom_call_target="tpu_custom_call" | custom-call | tf_op jit(solution)/shard_map/results/pallas_call | solution.py:917
